TPU v7x, 32 devices: a whole 2x2x4 slice. The times are simulated.
32 devices in a mesh: row: 4 (over x, core), col: 8 (over z, y).
Axes of the slice: x: 2, y: 2, z: 4, core: 2. Of those that a mesh axis runs over, the one named last changes fastest.
Arguments:
- amplitudes: float32 [2048, 256], P('row', 'col'), may hold values from -6 to 6
- integrals: float32 [256, 2048], P('row', 'col'), may hold values from -0.375 to 0.375
- occ_counts: int32 [8], replicated, may hold values from 1 to 10, 40 in all
- vir_counts: int32 [8], replicated, may hold values from 1 to 80, 400 in all
Outputs:
- symmetrized: float32 [2048, 2048], P('row', 'col')
Inputs may be any that keep to these rules, and one draw needn't show every extreme that they name: `occ_counts`: counts of occupied orbitals in the 8 irreducible representations, summing to 40. `vir_counts`: counts of virtual orbitals in the 8 irreducible representations, summing to 400.
All inputs are finite; a program needn't handle non-finite values.
Results may differ from a plain program's by a relative error of at most 0.00007.
Values sent between devices are 32-bit elements; how exact they have to be, the bound alone decides.
No kernel may reach another device: no remote copies, remote signals or barrier semaphores. Data moves between devices by JAX's collectives and lax.ppermute only.
A program may use at most 64 MiB of HBM per device.

v0:
```python
import jax
import jax.numpy as jnp
from jax import lax
from jax.sharding import PartitionSpec as P

NVIR = 400


def orbital_irreps(orbitals, counts):
    bounds = jnp.cumsum(counts)[:-1]
    return jnp.sum((orbitals[:, None] >= bounds[None, :]).astype(jnp.int32), axis=1)


def pair_labels(positions, occ_counts, vir_counts):
    occ_part = orbital_irreps(positions // NVIR, occ_counts)
    vir_part = orbital_irreps(positions % NVIR, vir_counts)
    return jnp.bitwise_xor(occ_part, vir_part)


def exact_dot(left, right):
    return jnp.dot(left, right, precision=lax.Precision.HIGHEST, preferred_element_type=jnp.float32)


def assemble(received, row_count, narrow):
    grouped = received.reshape(row_count, 2, -1).transpose(1, 0, 2).reshape(2, narrow, narrow)
    return grouped.transpose(1, 0, 2).reshape(narrow, 2 * narrow).T


def per_device(amplitudes, integrals, occ_counts, vir_counts):
    row_count = lax.axis_size("row")
    col_count = lax.axis_size("col")
    row_index = lax.axis_index("row")
    col_index = lax.axis_index("col")
    tall = amplitudes.shape[0]
    narrow = integrals.shape[1]
    row_labels = pair_labels(
        row_index * tall + jnp.arange(tall, dtype=jnp.int32), occ_counts, vir_counts
    )
    col_labels = pair_labels(
        col_index * narrow + jnp.arange(narrow, dtype=jnp.int32), occ_counts, vir_counts
    )
    allowed = row_labels[:, None] == col_labels[None, :]
    int_cols = lax.all_gather(integrals, "row", axis=0, tiled=True)
    product = exact_dot(lax.all_gather(amplitudes, "col", axis=1, tiled=True), int_cols)
    flattened = product.reshape(2, row_count, -1)
    outgoing = flattened.transpose(1, 0, 2).reshape(col_count, -1)
    section_one = lax.all_to_all(
        lax.all_to_all(outgoing, "row", split_axis=0, concat_axis=0, tiled=True),
        "col",
        split_axis=0,
        concat_axis=0,
        tiled=True,
    )
    section_two = lax.all_to_all(section_one, "row", split_axis=0, concat_axis=0, tiled=True)
    mirrored = assemble(section_two, row_count, narrow)
    return jnp.where(allowed, product + mirrored, 0.0)


def solution(mesh):
    placed = (P("row", "col"), P("row", "col"), P(), P())
    return jax.shard_map(
        per_device, mesh=mesh, in_specs=placed, out_specs=P("row", "col"), check_vma=False
    )
```

profile of v0, /device:TPU:0, one launch (start us, length us, event | category | flops | bytes accessed | tf_op | source)
XLA Modules:
  0.0 90.2 jit_solution(1421588870028163279)
XLA Ops:
  0.0 0.0 copy-start
  0.0 33.3 %all_gather.6 = f32[512,256]{0,1:T(8,128)S(1)} all-gather(f32[512,32]{0,1:T(8,128)} %param.4), channel_id=1, replica_groups=mesh['row'=4,'col'=8] {'col'}, dimensions={1}, use_global_device_ids=true | all-gather | bytes 589824 | tf_op jit(solution)/shard_map/all_gather | solution.py:44
  33.3 0.0 copy-done
  33.3 5.8 %all_gather.7 = f32[256,256]{1,0:T(8,128)S(1)} all-gather(f32[64,256]{1,0:T(8,128)S(1)} %copy-done), channel_id=1, replica_groups=mesh['row'=4,'col'=8] {'row'}, dimensions={0}, use_global_device_ids=true | all-gather | bytes 327680 | tf_op jit(solution)/shard_map/all_gather | solution.py:43
  39.1 1.0 %fusion.8 = f32[512,256]{1,0:T(8,128)S(1)} fusion(f32[512,256]{0,1:T(8,128)S(1)} %all_gather.6, f32[256,256]{1,0:T(8,128)S(1)} %all_gather.7), kind=kOutput, calls=%fused_computation.23 | convolution fusion | flops 402653184 | bytes 1310720 | tf_op jit(solution)/shard_map/dot_general | solution.py:21
  40.1 0.3 reshape.83
  40.4 0.4 copy.18
  40.8 11.4 %all_to_all.25 = f32[4,2,16384]{2,1,0:T(2,128)S(1)} all-to-all(f32[4,2,16384]{2,1,0:T(2,128)S(1)} %bitcast.20), channel_id=1, replica_groups=mesh['row'=4,'col'=8] {'row'}, dimensions={0} | all-to-all | bytes 1048576 | tf_op jit(solution)/shard_map/all_to_all | solution.py:48
  52.2 1.6 %all_to_all.21 = f32[8,1,16384]{2,1,0:T(1,128)} reshape(f32[4,2,16384]{2,1,0:T(2,128)S(1)} %all_to_all.25) | data formatting | bytes 1048576 | tf_op jit(solution)/shard_map/all_to_all | solution.py:47
  53.8 5.7 %all-to-all-start.1 = ((f32[8,1,16384]{2,1,0:T(1,128)}), f32[8,1,16384]{2,1,0:T(1,128)S(1)}, u32[]{:S(2)}, u32[]{:S(2)}) async-start(f32[8,1,16384]{2,1,0:T(1,128)} %all_to_all.21), calls=%async_computation.1 | async-start | bytes 1048576 | tf_op jit(solution)/shard_map/all_to_all | solution.py:47
  59.5 0.0 copy-start.1
  59.5 0.7 copy-done.1
  60.2 0.2 reduce-window.6
  60.4 0.0 copy-start.2
  60.4 0.7 copy-done.2
  61.0 0.2 reduce-window.9
  61.2 0.1 convert_reduce_fusion.3
  61.3 12.4 %all-to-all-done.1 = f32[8,1,16384]{2,1,0:T(1,128)S(1)} async-done(((f32[8,1,16384]{2,1,0:T(1,128)}), f32[8,1,16384]{2,1,0:T(1,128)S(1)}, u32[]{:S(2)}, u32[]{:S(2)}) %all-to-all-start.1) | async-done | bytes 524320 | tf_op jit(solution)/shard_map/all_to_all | solution.py:47
  73.7 1.2 %reduce = f32[8,16384]{1,0:T(8,128)S(1)} reduce(f32[8,1,16384]{2,1,0:T(1,128)S(1)} %all-to-all-done.1, f32[]{:T(128)} %constant.52), dimensions={1}, to_apply=%all_to_all.18.reduce_sub_computation | reduce | bytes 1048580 | tf_op jit(solution)/shard_map/all_to_all | solution.py:47
  74.9 1.1 %all_to_all.19 = f32[4,2,16384]{2,1,0:T(2,128)} reshape(f32[8,16384]{1,0:T(8,128)S(1)} %reduce) | data formatting | bytes 1048576 | tf_op jit(solution)/shard_map/all_to_all | solution.py:54
  76.0 3.5 %all-to-all-start.2 = ((f32[4,2,16384]{2,1,0:T(2,128)}), f32[4,2,16384]{2,1,0:T(2,128)S(1)}, u32[]{:S(2)}, u32[]{:S(2)}) async-start(f32[4,2,16384]{2,1,0:T(2,128)} %all_to_all.19), calls=%async_computation.2 | async-start | bytes 1048576 | tf_op jit(solution)/shard_map/all_to_all | solution.py:54
  79.5 0.1 convert_reduce_fusion.2
  79.6 0.1 convert_reduce_fusion.1
  79.7 0.1 convert_reduce_fusion
  79.8 8.5 %all-to-all-done.2 = f32[4,2,16384]{2,1,0:T(2,128)S(1)} async-done(((f32[4,2,16384]{2,1,0:T(2,128)}), f32[4,2,16384]{2,1,0:T(2,128)S(1)}, u32[]{:S(2)}, u32[]{:S(2)}) %all-to-all-start.2) | async-done | bytes 524320 | tf_op jit(solution)/shard_map/all_to_all | solution.py:54
  88.3 0.3 copy.14
  88.7 0.4 reshape.84
  89.0 0.2 copy.15
  89.2 0.9 %fusion = f32[512,256]{1,0:T(8,128)} fusion(f32[512,256]{1,0:T(8,128)S(1)} %fusion.8, f32[256,2,256]{0,2,1:T(8,128)S(1)} %copy.15, s32[256]{0:T(256)S(1)} %xor.15, s32[512]{0:T(512)S(1)} %xor.14), kind=kLoop, calls=%fused_computation.1 | loop fusion | flops 393216 | bytes 1575936 | tf_op jit(solution)/shard_map/jit(_where)/select_n | solution.py:56
  (6 shorter events, 0.0 us)
Async XLA Ops:
  0.0 33.3 %copy-start = (f32[64,256]{1,0:T(8,128)S(1)}, f32[64,256]{1,0:T(8,128)}, u32[]{:S(2)}) copy-start(f32[64,256]{1,0:T(8,128)} %param.5) | copy-start | bytes 196612
  53.8 19.9 %all-to-all-start.1 = ((f32[8,1,16384]{2,1,0:T(1,128)}), f32[8,1,16384]{2,1,0:T(1,128)S(1)}, u32[]{:S(2)}, u32[]{:S(2)}) async-start(f32[8,1,16384]{2,1,0:T(1,128)} %all_to_all.21), calls=%async_computation.1 | async-start | bytes 1048576 | tf_op jit(solution)/shard_map/all_to_all | solution.py:47
  59.5 0.7 copy-start.1
  60.4 0.7 copy-start.2
  76.0 12.3 %all-to-all-start.2 = ((f32[4,2,16384]{2,1,0:T(2,128)}), f32[4,2,16384]{2,1,0:T(2,128)S(1)}, u32[]{:S(2)}, u32[]{:S(2)}) async-start(f32[4,2,16384]{2,1,0:T(2,128)} %all_to_all.19), calls=%async_computation.2 | async-start | bytes 1048576 | tf_op jit(solution)/shard_map/all_to_all | solution.py:54
where the time goes:
time: 90.5 us; the launch traced here: 90.2 us
  blocking collectives  50.5 us (56%)
  waiting for transfers between devices  20.9 us (23%)
  starting transfers between devices  9.17 us (10%)
  local copies, waits for them, and re-layouts  5.58 us (6%)
  other arithmetic  2.92 us (3%)
  matrix products  1.01 us (1%)
    all_gather x1, blocking collectives, per_device(): lax.all_gather(amplitudes, 'col', axis=1, tiled=True)  33.3 us
    all_to_all x1, waiting for transfers between devices, per_device(): lax.all_to_all(lax.all_to_all(outgoing, 'row', split_axis=0, concat_axis=...  12.4 us
    all_to_all x1, blocking collectives, per_device(): lax.all_to_all(outgoing, 'row', split_axis=0, concat_axis=0, tiled=True)  11.4 us
    all_to_all x1, waiting for transfers between devices, per_device(): lax.all_to_all(section_one, 'row', split_axis=0, concat_axis=0, tiled=True)  8.52 us
    all_gather x1, blocking collectives, per_device(): int_cols = lax.all_gather(integrals, 'row', axis=0, tiled=True)  5.77 us
    all_to_all x1, starting transfers between devices, per_device(): lax.all_to_all(lax.all_to_all(outgoing, 'row', split_axis=0, concat_axis=...  5.7 us
    all_to_all x1, starting transfers between devices, per_device(): lax.all_to_all(section_one, 'row', split_axis=0, concat_axis=0, tiled=True)  3.47 us
  transfers between devices with their start and end apart: 2, of which 2 were waited for; matrix products, arithmetic and copies ran while one was open for 1% of the time, Pallas kernels for 0%

commit v1 on v0

v1 whole, which is shorter than its diff:
```python
import functools
import jax
import jax.numpy as jnp
from jax import lax
from jax.experimental import pallas as pl
from jax.experimental.pallas import tpu as pltpu
from jax.sharding import PartitionSpec as P

NVIR = 400
IRREPS = 8


def labels_of(pos, occ, vir):
    occ_of = pos // NVIR
    vir_of = pos - occ_of * NVIR
    one = jnp.zeros_like(pos)
    two = jnp.zeros_like(pos)
    for bound in occ:
        one = one + jnp.where(occ_of >= bound, 1, 0)
    for bound in vir:
        two = two + jnp.where(vir_of >= bound, 1, 0)
    return one ^ two


def finish(sizes, *refs):
    nr, nc, tall, narrow, ka, kb = sizes
    nz, nx = nc // 2, nr // 2
    occ_ref, vir_ref = refs[:2]
    a_refs = refs[2 : 2 + nc]
    refs = refs[2 + nc :]
    bm_refs, refs = refs[:nc], refs[nc:]
    b_refs, refs = refs[:nr], refs[nr:]
    ac_refs, refs = refs[:2], refs[2:]
    out_ref, left, right = refs
    row, col = lax.axis_index("row"), lax.axis_index("col")
    z, y = col // 2, lax.rem(col, 2)
    kw = ka * nc
    for d in range(nc):
        at = pl.multiple_of((col ^ d) * ka, ka)
        left[pl.ds(at, ka), :] = a_refs[d][...]
        at = pl.multiple_of(kw + (z ^ (d // 2)) * kb, kb)
        lane = pl.multiple_of((y ^ (d % 2)) * narrow, narrow)
        left[pl.ds(at, kb), pl.ds(lane, narrow)] = bm_refs[d][...]
    for d in range(nr):
        at = pl.multiple_of((row ^ d) * kb, kb)
        right[pl.ds(at, kb), :] = b_refs[d][...]
    for d in range(nc):
        at = pl.multiple_of(kw + (col ^ d) * ka, ka)
        rows = pl.ds(d * ka, ka)
        right[pl.ds(at, ka), :] = ac_refs[0][rows, :] + ac_refs[1][rows, :]
    lw = left[...]
    rw = right[...]
    lh = lw.astype(jnp.bfloat16)
    ll = (lw - lh.astype(jnp.float32)).astype(jnp.bfloat16)
    rh = rw.astype(jnp.bfloat16)
    rl = (rw - rh.astype(jnp.float32)).astype(jnp.bfloat16)

    def mm(one, two):
        return lax.dot_general(one, two, (((0,), (0,)), ((), ())), preferred_element_type=jnp.float32)

    total = mm(lh, rl) + mm(ll, rh) + mm(lh, rh)
    occ, vir = [], []
    one = two = 0
    for h in range(IRREPS - 1):
        one, two = one + occ_ref[h], two + vir_ref[h]
        occ.append(one)
        vir.append(two)
    rl_ = labels_of(row * tall + lax.broadcasted_iota(jnp.int32, (tall, 1), 0), occ, vir)
    cl_ = labels_of(col * narrow + lax.broadcasted_iota(jnp.int32, (1, narrow), 1), occ, vir)
    out_ref[...] = jnp.where(rl_ == cl_, total, 0.0)


def per_device(sizes, amplitudes, integrals, occ_counts, vir_counts):
    nr, nc, tall, narrow, ka, kb = sizes
    nz, nx = nc // 2, nr // 2
    row, col = lax.axis_index("row"), lax.axis_index("col")
    z, y = col // 2, lax.rem(col, 2)

    def send(value, pairs):
        return lax.ppermute(value, ("row", "col"), pairs)

    def moved(dr, dc, keep=lambda r, c: True):
        return [(r * nc + c, (r ^ dr) * nc + (c ^ dc)) for r in range(nr) for c in range(nc) if keep(r, c)]

    mirror = [(zz * nc + 2 * r + h, r * nc + 2 * zz + h) for r in range(nr) for zz in range(nz) for h in range(2)]
    at = amplitudes.T
    a = [None] * nc
    a[0] = at
    for d in range(nz - 1, 0, -1):
        a[2 * d] = send(at, moved(0, 2 * d))
    bm = send(integrals, mirror)
    b = [None] * nr
    b[0] = integrals
    for d in range(2, nr, 2):
        b[d] = send(integrals, moved(d, 0))
    for d in range(0, nr, 2):
        b[d + 1] = send(b[d], moved(1, 0))
    m = [None] * nc
    m[0] = bm
    for d in range(nz - 1, 0, -1):
        m[2 * d] = send(bm, moved(0, 2 * d))
    ay = send(jnp.concatenate(a[0::2], 0), moved(0, 1))
    for d in range(nz):
        a[2 * d + 1] = ay[d * ka : (d + 1) * ka]
    my = send(jnp.concatenate(m[0::2], 0), moved(0, 1))
    for d in range(nz):
        m[2 * d + 1] = my[d * kb : (d + 1) * kb]
    own = jnp.concatenate([lax.dynamic_slice_in_dim(v, y * narrow, narrow, 1) for v in a], axis=0)
    own = jnp.where(row == z, own, 0.0)
    own = lax.optimization_barrier((own, *m[2::2], *b))[0]
    acx = own
    for d in range(2, nr, 2):
        acx = acx + send(own, moved(d, 0, lambda r, c: r == c // 2))
    acx = lax.optimization_barrier((acx, *m[1::2]))[0]
    ack = send(acx, moved(1, 0, lambda r, c: r % 2 == (c // 2) % 2))
    smem = pl.BlockSpec(memory_space=pltpu.SMEM)
    vmem = pl.BlockSpec(memory_space=pltpu.VMEM)
    return pl.pallas_call(
        functools.partial(finish, sizes),
        out_shape=jax.ShapeDtypeStruct((tall, narrow), jnp.float32),
        in_specs=[smem, smem] + [vmem] * (2 * nc + nr + 2),
        out_specs=vmem,
        scratch_shapes=[
            pltpu.VMEM((ka * nc + kb * nr, tall), jnp.float32),
            pltpu.VMEM((ka * nc + kb * nr, narrow), jnp.float32),
        ],
        compiler_params=pltpu.CompilerParams(vmem_limit_bytes=40 * 1024 * 1024),
    )(occ_counts, vir_counts, *a, *m, *b, acx, ack)


def solution(mesh):
    nr, nc = mesh.shape["row"], mesh.shape["col"]

    def whole(amplitudes, integrals, occ_counts, vir_counts):
        pairs, kw = amplitudes.shape
        sizes = (nr, nc, pairs // nr, pairs // nc, kw // nc, kw // nr)
        placed = (P("row", "col"), P("row", "col"), P(), P())
        return jax.shard_map(
            functools.partial(per_device, sizes), mesh=mesh, in_specs=placed, out_specs=P("row", "col"), check_vma=False
        )(amplitudes, integrals, occ_counts, vir_counts)

    return whole
```

time: 90.5 us -> 37 us (0.41)
  blocking collectives: 50.5 us -> 0 us
  starting transfers between devices: 9.17 us -> 19.3 us
  waiting for transfers between devices: 20.9 us -> 13.5 us
  local copies, waits for them, and re-layouts: 5.58 us -> 0.14 us
  Pallas kernels: 0 us -> 2.51 us
  other arithmetic: 2.92 us -> 1.01 us
  matrix products: 1.01 us -> 0 us
    all_gather x2 -> x0, blocking collectives: 39.1 us -> none  [the longest x1 33.3 us: per_device(): lax.all_gather(amplitudes, 'col', axis=1, tiled=True)]
    all_to_all x2 -> x0, waiting for transfers between devices: 20.9 us -> none  [the longest x1 12.4 us: per_device(): lax.all_to_all(lax.all_to_all(outgoing, 'row', split_axis=0, concat_axis=...]
    ppermute x0 -> x14, starting transfers between devices: none -> 19.3 us  [send(): return lax.ppermute(value, ('row', 'col'), pairs)]
    ppermute x0 -> x14, waiting for transfers between devices: none -> 13.5 us  [send(): return lax.ppermute(value, ('row', 'col'), pairs)]
    all_to_all x1 -> x0, blocking collectives: 11.4 us -> none  [per_device(): lax.all_to_all(outgoing, 'row', split_axis=0, concat_axis=0, tiled=True)]
    all_to_all x2 -> x0, starting transfers between devices: 9.17 us -> none  [the longest x1 5.7 us: per_device(): lax.all_to_all(lax.all_to_all(outgoing, 'row', split_axis=0, concat_axis=...]
    all_to_all x2 -> x0, local copies, waits for them, and re-layouts: 2.7 us -> none  [the longest x1 1.6 us: per_device(): lax.all_to_all(lax.all_to_all(outgoing, 'row', split_axis=0, concat_axis=...]
    pallas_call x0 -> x1, Pallas kernels: none -> 2.51 us  [per_device(): pl.pallas_call(functools.partial(finish, sizes), out_shape=jax.ShapeDtype...]
  transfers between devices with their start and end apart: 2 -> 14, of which waited for: 2 -> 6; matrix products, arithmetic and copies ran while one was open for 1% -> 3% of each run, Pallas kernels for 0% -> 0%
where the time goes in v1:
time: 37 us; the launch traced here: 36.7 us
  starting transfers between devices  19.3 us (52%)
  waiting for transfers between devices  13.5 us (36%)
  Pallas kernels  2.51 us (7%)
  other arithmetic  1.01 us (3%)
    ppermute x14, starting transfers between devices, send(): return lax.ppermute(value, ('row', 'col'), pairs)  19.3 us
    ppermute x14, waiting for transfers between devices, send(): return lax.ppermute(value, ('row', 'col'), pairs)  13.5 us
    pallas_call x1, Pallas kernels, per_device(): pl.pallas_call(functools.partial(finish, sizes), out_shape=jax.ShapeDtype...  2.51 us
    concatenate x1, other arithmetic, per_device(): ay = send(jnp.concatenate(a[0::2], 0), moved(0, 1))  0.93 us
  transfers between devices with their start and end apart: 14, of which 6 were waited for; matrix products, arithmetic and copies ran while one was open for 3% of the time, Pallas kernels for 0%

profile of v1, /device:TPU:0, one launch (start us, length us, event | category | flops | bytes accessed | tf_op | source)
XLA Modules:
  0.0 36.7 jit_solution(5093937553444552133)
XLA Ops:
  0.0 0.0 copy-start.1
  0.0 5.0 %collective-permute-start.2 = (f32[32,512]{1,0:T(8,128)}, f32[32,512]{1,0:T(8,128)S(1)}, u32[]{:S(2)}, u32[]{:S(2)}) collective-permute-start(f32[32,512]{1,0:T(8,128)} %bitcast.3), channel_id=1, source_target_pairs={{0,6},{1,7},{2,4},{3,5},{4,2},{5,3},{6,0},{7,1},{8,14},{9,15},{10,... | collective-permute-start | bytes 196616 | tf_op jit(solution)/shard_map/ppermute | solution.py:80
  5.1 0.0 collective-permute-start.1
  5.1 0.6 %collective-permute-start = (f32[32,512]{1,0:T(8,128)}, f32[32,512]{1,0:T(8,128)S(1)}, u32[]{:S(2)}, u32[]{:S(2)}) collective-permute-start(f32[32,512]{1,0:T(8,128)} %bitcast.5), channel_id=1, source_target_pairs={{0,2},{1,3},{2,0},{3,1},{4,6},{5,7},{6,4},{7,5},{8,10},{9,11},{10,... | collective-permute-start | bytes 196616 | tf_op jit(solution)/shard_map/ppermute | solution.py:80
  5.7 1.5 %collective-permute-start.4 = (f32[64,256]{1,0:T(8,128)}, f32[64,256]{1,0:T(8,128)S(1)}, u32[]{:S(2)}, u32[]{:S(2)}) collective-permute-start(f32[64,256]{1,0:T(8,128)} %refs_18_.1), channel_id=1, source_target_pairs={{0,0},{1,1},{8,2},{9,3},{16,4},{17,5},{24,6},{25,7},{2,8},{3,9},{1... | collective-permute-start | bytes 196616 | tf_op jit(solution)/shard_map/ppermute | solution.py:80
  7.2 0.7 %collective-permute-done.2.refs_8_ = f32[32,512]{1,0:T(8,128)S(1)} collective-permute-done((f32[32,512]{1,0:T(8,128)}, f32[32,512]{1,0:T(8,128)S(1)}, u32[]{:S(2)}, u32[]{:S(2)}) %collective-permute-start.2) | collective-permute-done | bytes 65568 | tf_op jit(solution)/shard_map/ppermute | solution.py:80
  7.9 3.0 %collective-permute-done.1.refs_6_ = f32[32,512]{1,0:T(8,128)S(1)} collective-permute-done((f32[32,512]{1,0:T(8,128)}, f32[32,512]{1,0:T(8,128)S(1)}, u32[]{:S(2)}, u32[]{:S(2)}) %collective-permute-start.1) | collective-permute-done | bytes 65568 | tf_op jit(solution)/shard_map/ppermute | solution.py:80
  10.9 0.0 collective-permute-done.refs_4_
  10.9 0.0 copy-start
  10.9 0.9 %pad_maximum_fusion = f32[128,512]{1,0:T(8,128)S(1)} fusion(f32[32,512]{1,0:T(8,128)S(1)} %collective-permute-done.2.refs_8_, f32[32,512]{1,0:T(8,128)S(1)} %collective-permute-done.1.refs_6_, f32[32,512]{1,0:T(8,128)S(1)} %collective-permute-done.refs_4_, f32[32,512]{1,0:T(8,128)} %bitcast.6), kind=kLoop, calls=%fused_computation | loop fusion | flops 196608 | bytes 524288 | tf_op jit(solution)/shard_map/concatenate | solution.py:102
  11.8 1.6 %collective-permute-start.3 = (f32[128,512]{1,0:T(8,128)S(1)}, f32[128,512]{1,0:T(8,128)S(1)}, u32[]{:S(2)}, u32[]{:S(2)}) collective-permute-start(f32[128,512]{1,0:T(8,128)S(1)} %pad_maximum_fusion), channel_id=1, source_target_pairs={{0,1},{1,0},{2,3},{3,2},{4,5},{5,4},{6,7},{7,6},{8,9},{9,8},{10,11... | collective-permute-start | bytes 786440 | tf_op jit(solution)/shard_map/ppermute | solution.py:80
  13.4 0.0 copy-done.1
  13.4 1.5 %collective-permute-start.10 = (f32[64,256]{1,0:T(8,128)S(1)}, f32[64,256]{1,0:T(8,128)S(1)}, u32[]{:S(2)}, u32[]{:S(2)}) collective-permute-start(f32[64,256]{1,0:T(8,128)S(1)} %copy-done.1), channel_id=1, source_target_pairs={{0,16},{1,17},{2,18},{3,19},{4,20},{5,21},{6,22},{7,23},{8,24},{9,... | collective-permute-start | bytes 196616 | tf_op jit(solution)/shard_map/ppermute | solution.py:80
  14.9 0.0 collective-permute-done.4.refs_10_
  14.9 3.1 %collective-permute-start.7 = (f32[64,256]{1,0:T(8,128)S(1)}, f32[64,256]{1,0:T(8,128)S(1)}, u32[]{:S(2)}, u32[]{:S(2)}) collective-permute-start(f32[64,256]{1,0:T(8,128)S(1)} %collective-permute-done.4.refs_10_), channel_id=1, source_target_pairs={{0,6},{1,7},{2,4},{3,5},{4,2},{5,3},{6,0},{7,1},{8,14},{9,15},{10,... | collective-permute-start | bytes 196616 | tf_op jit(solution)/shard_map/ppermute | solution.py:80
  18.0 0.0 collective-permute-start.6
  18.0 1.2 %collective-permute-start.5 = (f32[64,256]{1,0:T(8,128)S(1)}, f32[64,256]{1,0:T(8,128)S(1)}, u32[]{:S(2)}, u32[]{:S(2)}) collective-permute-start(f32[64,256]{1,0:T(8,128)S(1)} %collective-permute-done.4.refs_10_), channel_id=1, source_target_pairs={{0,2},{1,3},{2,0},{3,1},{4,6},{5,7},{6,4},{7,5},{8,10},{9,11},{10,... | collective-permute-start | bytes 196616 | tf_op jit(solution)/shard_map/ppermute | solution.py:80
  19.3 0.0 copy-done
  19.3 0.0 collective-permute-done.10.refs_20_
  19.3 0.1 collective-permute-start.9
  19.4 2.3 %collective-permute-done.7.refs_16_ = f32[64,256]{1,0:T(8,128)S(1)} collective-permute-done((f32[64,256]{1,0:T(8,128)S(1)}, f32[64,256]{1,0:T(8,128)S(1)}, u32[]{:S(2)}, u32[]{:S(2)}) %collective-permute-start.7) | collective-permute-done | bytes 65568 | tf_op jit(solution)/shard_map/ppermute | solution.py:80
  21.7 0.0 collective-permute-start.11
  21.7 2.2 %collective-permute-done.6.refs_14_ = f32[64,256]{1,0:T(8,128)S(1)} collective-permute-done((f32[64,256]{1,0:T(8,128)S(1)}, f32[64,256]{1,0:T(8,128)S(1)}, u32[]{:S(2)}, u32[]{:S(2)}) %collective-permute-start.6) | collective-permute-done | bytes 65568 | tf_op jit(solution)/shard_map/ppermute | solution.py:80
  23.9 0.0 collective-permute-done.5.refs_12_
  23.9 0.9 %collective-permute-start.8 = (f32[256,256]{1,0:T(8,128)S(1)}, f32[256,256]{1,0:T(8,128)S(1)}, u32[]{:S(2)}, u32[]{:S(2)}) collective-permute-start(f32[256,256]{1,0:T(8,128)S(1)} %pad_maximum_fusion.1), channel_id=1, source_target_pairs={{0,1},{1,0},{2,3},{3,2},{4,5},{5,4},{6,7},{7,6},{8,9},{9,8},{10,11... | collective-permute-start | bytes 786440 | tf_op jit(solution)/shard_map/ppermute | solution.py:80
  24.8 0.0 collective-permute-done.3
  25.0 0.0 collective-permute-done.9.refs_19_
  25.0 0.0 collective-permute-done.11.refs_21_
  25.0 2.4 %collective-permute-start.12 = (f32[256,256]{1,0:T(8,128)S(1)}, f32[256,256]{1,0:T(8,128)S(1)}, u32[]{:S(2)}, u32[]{:S(2)}) collective-permute-start(f32[256,256]{1,0:T(8,128)S(1)} %broadcast_select_fusion), channel_id=1, source_target_pairs={{0,16},{1,17},{10,26},{11,27},{20,4},{21,5},{30,14},{31,15}} | collective-permute-start | bytes 786440 | tf_op jit(solution)/shard_map/ppermute | solution.py:80
  27.5 4.1 %collective-permute-done.8 = f32[256,256]{1,0:T(8,128)S(1)} collective-permute-done((f32[256,256]{1,0:T(8,128)S(1)}, f32[256,256]{1,0:T(8,128)S(1)}, u32[]{:S(2)}, u32[]{:S(2)}) %collective-permute-start.8) | collective-permute-done | bytes 262176 | tf_op jit(solution)/shard_map/ppermute | solution.py:80
  31.6 0.0 collective-permute-done.12
  31.7 0.0 copy-start.2
  31.7 0.0 copy-start.3
  31.7 1.3 %collective-permute-start.13 = (f32[256,256]{1,0:T(8,128)S(1)}, f32[256,256]{1,0:T(8,128)S(1)}, u32[]{:S(2)}, u32[]{:S(2)}) collective-permute-start(f32[256,256]{1,0:T(8,128)S(1)} %add.6.refs_22_), channel_id=1, source_target_pairs={{0,8},{1,9},{4,12},{5,13},{10,2},{11,3},{14,6},{15,7},{16,24},{17,... | collective-permute-start | bytes 786440 | tf_op jit(solution)/shard_map/ppermute | solution.py:80
  33.0 1.1 %collective-permute-done.13.refs_23_ = f32[256,256]{1,0:T(8,128)S(1)} collective-permute-done((f32[256,256]{1,0:T(8,128)S(1)}, f32[256,256]{1,0:T(8,128)S(1)}, u32[]{:S(2)}, u32[]{:S(2)}) %collective-permute-start.13) | collective-permute-done | bytes 262176 | tf_op jit(solution)/shard_map/ppermute | solution.py:80
  34.1 0.0 copy-done.2
  34.1 0.0 copy-done.3
  34.2 2.5 %shard_map.46 = f32[512,256]{1,0:T(8,128)} custom-call(s32[8]{0:T(128)S(1)} %copy-done.2, s32[8]{0:T(128)S(1)} %copy-done.3, f32[32,512]{1,0:T(8,128)S(1)} %bitcast.7, f32[32,512]{1,0:T(8,128)S(1)} %get-tuple-element.16.refs_3_, f32[32,512]{1,0:T(8,128)S(1)} %collective-permute-done.refs_4_, f32[32,512]{1,0:T(8,128)S(1)} %get-tuple-element.15.refs_5_, ...), custom_call_target="tpu_custom_call" | custom-call | tf_op jit(solution)/shard_map/pallas_call | solution.py:118
  (13 shorter events, 0.2 us)
Async XLA Ops:
  0.0 13.4 %copy-start.1 = (f32[64,256]{1,0:T(8,128)S(1)}, f32[64,256]{1,0:T(8,128)}, u32[]{:S(2)}) copy-start(f32[64,256]{1,0:T(8,128)} %refs_18_.1) | copy-start | bytes 196612
  0.0 7.9 %collective-permute-start.2 = (f32[32,512]{1,0:T(8,128)}, f32[32,512]{1,0:T(8,128)S(1)}, u32[]{:S(2)}, u32[]{:S(2)}) collective-permute-start(f32[32,512]{1,0:T(8,128)} %bitcast.3), channel_id=1, source_target_pairs={{0,6},{1,7},{2,4},{3,5},{4,2},{5,3},{6,0},{7,1},{8,14},{9,15},{10,... | collective-permute-start | bytes 196616 | tf_op jit(solution)/shard_map/ppermute | solution.py:80
  5.1 5.8 %collective-permute-start.1 = (f32[32,512]{1,0:T(8,128)}, f32[32,512]{1,0:T(8,128)S(1)}, u32[]{:S(2)}, u32[]{:S(2)}) collective-permute-start(f32[32,512]{1,0:T(8,128)} %bitcast.4), channel_id=1, source_target_pairs={{0,4},{1,5},{2,6},{3,7},{4,0},{5,1},{6,2},{7,3},{8,12},{9,13},{10,... | collective-permute-start | bytes 196616 | tf_op jit(solution)/shard_map/ppermute | solution.py:80
  5.1 5.8 %collective-permute-start = (f32[32,512]{1,0:T(8,128)}, f32[32,512]{1,0:T(8,128)S(1)}, u32[]{:S(2)}, u32[]{:S(2)}) collective-permute-start(f32[32,512]{1,0:T(8,128)} %bitcast.5), channel_id=1, source_target_pairs={{0,2},{1,3},{2,0},{3,1},{4,6},{5,7},{6,4},{7,5},{8,10},{9,11},{10,... | collective-permute-start | bytes 196616 | tf_op jit(solution)/shard_map/ppermute | solution.py:80
  5.7 9.2 %collective-permute-start.4 = (f32[64,256]{1,0:T(8,128)}, f32[64,256]{1,0:T(8,128)S(1)}, u32[]{:S(2)}, u32[]{:S(2)}) collective-permute-start(f32[64,256]{1,0:T(8,128)} %refs_18_.1), channel_id=1, source_target_pairs={{0,0},{1,1},{8,2},{9,3},{16,4},{17,5},{24,6},{25,7},{2,8},{3,9},{1... | collective-permute-start | bytes 196616 | tf_op jit(solution)/shard_map/ppermute | solution.py:80
  10.9 8.4 %copy-start = (f32[512,32]{0,1:T(8,128)S(1)}, f32[512,32]{0,1:T(8,128)}, u32[]{:S(2)}) copy-start(f32[512,32]{0,1:T(8,128)} %param.4) | copy-start | bytes 196612
  11.8 13.0 %collective-permute-start.3 = (f32[128,512]{1,0:T(8,128)S(1)}, f32[128,512]{1,0:T(8,128)S(1)}, u32[]{:S(2)}, u32[]{:S(2)}) collective-permute-start(f32[128,512]{1,0:T(8,128)S(1)} %pad_maximum_fusion), channel_id=1, source_target_pairs={{0,1},{1,0},{2,3},{3,2},{4,5},{5,4},{6,7},{7,6},{8,9},{9,8},{10,11... | collective-permute-start | bytes 786440 | tf_op jit(solution)/shard_map/ppermute | solution.py:80
  13.4 5.9 %collective-permute-start.10 = (f32[64,256]{1,0:T(8,128)S(1)}, f32[64,256]{1,0:T(8,128)S(1)}, u32[]{:S(2)}, u32[]{:S(2)}) collective-permute-start(f32[64,256]{1,0:T(8,128)S(1)} %copy-done.1), channel_id=1, source_target_pairs={{0,16},{1,17},{2,18},{3,19},{4,20},{5,21},{6,22},{7,23},{8,24},{9,... | collective-permute-start | bytes 196616 | tf_op jit(solution)/shard_map/ppermute | solution.py:80
  14.9 6.8 %collective-permute-start.7 = (f32[64,256]{1,0:T(8,128)S(1)}, f32[64,256]{1,0:T(8,128)S(1)}, u32[]{:S(2)}, u32[]{:S(2)}) collective-permute-start(f32[64,256]{1,0:T(8,128)S(1)} %collective-permute-done.4.refs_10_), channel_id=1, source_target_pairs={{0,6},{1,7},{2,4},{3,5},{4,2},{5,3},{6,0},{7,1},{8,14},{9,15},{10,... | collective-permute-start | bytes 196616 | tf_op jit(solution)/shard_map/ppermute | solution.py:80
  18.0 5.9 %collective-permute-start.6 = (f32[64,256]{1,0:T(8,128)S(1)}, f32[64,256]{1,0:T(8,128)S(1)}, u32[]{:S(2)}, u32[]{:S(2)}) collective-permute-start(f32[64,256]{1,0:T(8,128)S(1)} %collective-permute-done.4.refs_10_), channel_id=1, source_target_pairs={{0,4},{1,5},{2,6},{3,7},{4,0},{5,1},{6,2},{7,3},{8,12},{9,13},{10,... | collective-permute-start | bytes 196616 | tf_op jit(solution)/shard_map/ppermute | solution.py:80
  18.0 5.9 %collective-permute-start.5 = (f32[64,256]{1,0:T(8,128)S(1)}, f32[64,256]{1,0:T(8,128)S(1)}, u32[]{:S(2)}, u32[]{:S(2)}) collective-permute-start(f32[64,256]{1,0:T(8,128)S(1)} %collective-permute-done.4.refs_10_), channel_id=1, source_target_pairs={{0,2},{1,3},{2,0},{3,1},{4,6},{5,7},{6,4},{7,5},{8,10},{9,11},{10,... | collective-permute-start | bytes 196616 | tf_op jit(solution)/shard_map/ppermute | solution.py:80
  19.3 5.7 %collective-permute-start.9 = (f32[64,256]{1,0:T(8,128)S(1)}, f32[64,256]{1,0:T(8,128)S(1)}, u32[]{:S(2)}, u32[]{:S(2)}) collective-permute-start(f32[64,256]{1,0:T(8,128)S(1)} %copy-done.1), channel_id=1, source_target_pairs={{0,8},{1,9},{2,10},{3,11},{4,12},{5,13},{6,14},{7,15},{8,0},{9,1},... | collective-permute-start | bytes 196616 | tf_op jit(solution)/shard_map/ppermute | solution.py:80
  21.7 3.4 %collective-permute-start.11 = (f32[64,256]{1,0:T(8,128)S(1)}, f32[64,256]{1,0:T(8,128)S(1)}, u32[]{:S(2)}, u32[]{:S(2)}) collective-permute-start(f32[64,256]{1,0:T(8,128)S(1)} %collective-permute-done.10.refs_20_), channel_id=1, source_target_pairs={{0,8},{1,9},{2,10},{3,11},{4,12},{5,13},{6,14},{7,15},{8,0},{9,1},... | collective-permute-start | bytes 196616 | tf_op jit(solution)/shard_map/ppermute | solution.py:80
  23.9 7.7 %collective-permute-start.8 = (f32[256,256]{1,0:T(8,128)S(1)}, f32[256,256]{1,0:T(8,128)S(1)}, u32[]{:S(2)}, u32[]{:S(2)}) collective-permute-start(f32[256,256]{1,0:T(8,128)S(1)} %pad_maximum_fusion.1), channel_id=1, source_target_pairs={{0,1},{1,0},{2,3},{3,2},{4,5},{5,4},{6,7},{7,6},{8,9},{9,8},{10,11... | collective-permute-start | bytes 786440 | tf_op jit(solution)/shard_map/ppermute | solution.py:80
  25.0 6.6 %collective-permute-start.12 = (f32[256,256]{1,0:T(8,128)S(1)}, f32[256,256]{1,0:T(8,128)S(1)}, u32[]{:S(2)}, u32[]{:S(2)}) collective-permute-start(f32[256,256]{1,0:T(8,128)S(1)} %broadcast_select_fusion), channel_id=1, source_target_pairs={{0,16},{1,17},{10,26},{11,27},{20,4},{21,5},{30,14},{31,15}} | collective-permute-start | bytes 786440 | tf_op jit(solution)/shard_map/ppermute | solution.py:80
  31.7 2.5 %copy-start.2 = (s32[8]{0:T(128)S(1)}, s32[8]{0:T(128)}, u32[]{:S(2)}) copy-start(s32[8]{0:T(128)} %refs_0_.1) | copy-start | bytes 100
  31.7 2.5 %copy-start.3 = (s32[8]{0:T(128)S(1)}, s32[8]{0:T(128)}, u32[]{:S(2)}) copy-start(s32[8]{0:T(128)} %refs_1_.1) | copy-start | bytes 100
  31.7 2.4 %collective-permute-start.13 = (f32[256,256]{1,0:T(8,128)S(1)}, f32[256,256]{1,0:T(8,128)S(1)}, u32[]{:S(2)}, u32[]{:S(2)}) collective-permute-start(f32[256,256]{1,0:T(8,128)S(1)} %add.6.refs_22_), channel_id=1, source_target_pairs={{0,8},{1,9},{4,12},{5,13},{10,2},{11,3},{14,6},{15,7},{16,24},{17,... | collective-permute-start | bytes 786440 | tf_op jit(solution)/shard_map/ppermute | solution.py:80

commit v2 on v1

v2 whole, which is shorter than its diff:
```python
import functools
import jax
import jax.numpy as jnp
from jax import lax
from jax.experimental import pallas as pl
from jax.experimental.pallas import tpu as pltpu
from jax.sharding import PartitionSpec as P

NVIR = 400
IRREPS = 8


def labels_of(pos, occ, vir):
    occ_of = pos // NVIR
    vir_of = pos - occ_of * NVIR
    one = jnp.zeros_like(pos)
    two = jnp.zeros_like(pos)
    for bound in occ:
        one = one + jnp.where(occ_of >= bound, 1, 0)
    for bound in vir:
        two = two + jnp.where(vir_of >= bound, 1, 0)
    return one ^ two


def halves(value):
    high = value.astype(jnp.bfloat16)
    return high, (value - high.astype(jnp.float32)).astype(jnp.bfloat16)


def product(left, right):
    def mm(one, two):
        return lax.dot_general(one, two, (((0,), (0,)), ((), ())), preferred_element_type=jnp.float32)

    (lh, ll), (rh, rl) = halves(left), halves(right)
    return mm(lh, rl) + mm(ll, rh) + mm(lh, rh)


def direct(sizes, *refs):
    nr, nc, tall, narrow, ka, kb = sizes
    occ_ref, vir_ref = refs[:2]
    a_refs, b_refs = refs[2 : 2 + nc], refs[2 + nc : 2 + nc + nr]
    out_ref, mask_ref, left, right = refs[2 + nc + nr :]
    row, col = lax.axis_index("row"), lax.axis_index("col")
    for d in range(nc):
        left[pl.ds(pl.multiple_of((col ^ d) * ka, ka), ka), :] = a_refs[d][...]
    for d in range(nr):
        right[pl.ds(pl.multiple_of((row ^ d) * kb, kb), kb), :] = b_refs[d][...]
    out_ref[...] = product(left[...], right[...])
    occ, vir = [], []
    one = two = 0
    for h in range(IRREPS - 1):
        one, two = one + occ_ref[h], two + vir_ref[h]
        occ.append(one)
        vir.append(two)
    rows = labels_of(row * tall + lax.broadcasted_iota(jnp.int32, (tall, 1), 0), occ, vir)
    cols = labels_of(col * narrow + lax.broadcasted_iota(jnp.int32, (1, narrow), 1), occ, vir)
    mask_ref[...] = jnp.where(rows == cols, 1.0, 0.0)


def mirrored(sizes, *refs):
    nr, nc, tall, narrow, ka, kb = sizes
    nz = nc // 2
    part_ref, mask_ref = refs[:2]
    m_refs, ac_refs = refs[2 : 2 + nc], refs[2 + nc : 4 + nc]
    out_ref, left, right = refs[4 + nc :]
    col = lax.axis_index("col")
    z, y = col // 2, lax.rem(col, 2)
    for d in range(nc):
        at = pl.multiple_of((z ^ (d // 2)) * kb, kb)
        lane = pl.multiple_of((y ^ (d % 2)) * narrow, narrow)
        left[pl.ds(at, kb), pl.ds(lane, narrow)] = m_refs[d][...]
        at = pl.multiple_of((col ^ d) * ka, ka)
        rows = pl.ds((d % 2 * nz + d // 2) * ka, ka)
        right[pl.ds(at, ka), :] = ac_refs[0][rows, :] + ac_refs[1][rows, :]
    total = part_ref[...] + product(left[...], right[...])
    out_ref[...] = jnp.where(mask_ref[...] > 0.0, total, 0.0)


def per_device(sizes, amplitudes, integrals, occ_counts, vir_counts):
    nr, nc, tall, narrow, ka, kb = sizes
    nz = nc // 2
    row, col = lax.axis_index("row"), lax.axis_index("col")
    z, y = col // 2, lax.rem(col, 2)

    def send(value, pairs):
        return lax.ppermute(value, ("row", "col"), pairs)

    def moved(dr, dc, keep=lambda r, c: True):
        return [(r * nc + c, (r ^ dr) * nc + (c ^ dc)) for r in range(nr) for c in range(nc) if keep(r, c)]

    def mirror(e):
        return [(r * nc + c, (c // 2) * nc + 2 * (r ^ e) + c % 2) for r in range(nr) for c in range(nc)]

    def after(value, *others):
        return lax.optimization_barrier((value, *others))[0]

    def half_of(chunks, part):
        return jnp.concatenate([lax.dynamic_slice_in_dim(v, part * narrow, narrow, 1) for v in chunks], axis=0)

    def home(r, c):
        return r == c // 2

    def core(r, c):
        return r % 2 == (c // 2) % 2

    at = amplitudes.T
    a = [None] * nc
    a[0] = at
    m = [None] * nc
    b = [None] * nr
    b[0] = integrals
    for d in range(nz - 1, 0, -1):
        a[2 * d] = send(at, moved(0, 2 * d))
    for e in range(0, nz, 2):
        m[2 * e] = send(integrals, mirror(e))
    for d in range(2, nr, 2):
        b[d] = send(after(integrals, *a[2::2]), moved(d, 0))
    ay = send(jnp.concatenate(a[0::2], 0), moved(0, 1))
    for d in range(nz):
        a[2 * d + 1] = ay[d * ka : (d + 1) * ka]
    mz = send(jnp.concatenate(m[0::4], 0), moved(0, 2))
    for i in range(nz // 2):
        m[4 * i + 2] = mz[i * kb : (i + 1) * kb]
    bk = send(jnp.concatenate(b[0::2], 0), moved(1, 0))
    for d in range(0, nr, 2):
        b[d + 1] = bk[d // 2 * kb : (d // 2 + 1) * kb]
    px = half_of(a[0::2], y)
    px = sum(send(px, moved(d, 0, home)) for d in range(2, nr, 2))
    pxy = after(half_of(a[0::2], 1 - y), *a[2::2])
    pxy = sum(send(pxy, moved(d, 1, home)) for d in range(2, nr, 2))
    my = send(jnp.concatenate(m[0::2], 0), moved(0, 1))
    for d in range(nz):
        m[2 * d + 1] = my[d * kb : (d + 1) * kb]
    acx = jnp.where(row == z, half_of(a[0::2] + a[1::2], y), jnp.concatenate([px, pxy], axis=0))
    ack = send(acx, moved(1, 0, core))

    smem = pl.BlockSpec(memory_space=pltpu.SMEM)
    vmem = pl.BlockSpec(memory_space=pltpu.VMEM)
    limit = pltpu.CompilerParams(vmem_limit_bytes=40 * 1024 * 1024)
    tile = jax.ShapeDtypeStruct((tall, narrow), jnp.float32)
    part, mask = pl.pallas_call(
        functools.partial(direct, sizes),
        out_shape=(tile, tile),
        in_specs=[smem, smem] + [vmem] * (nc + nr),
        out_specs=(vmem, vmem),
        scratch_shapes=[pltpu.VMEM((ka * nc, tall), jnp.float32), pltpu.VMEM((kb * nr, narrow), jnp.float32)],
        compiler_params=limit,
    )(occ_counts, vir_counts, *a, *b)
    return pl.pallas_call(
        functools.partial(mirrored, sizes),
        out_shape=tile,
        in_specs=[vmem] * (4 + nc),
        out_specs=vmem,
        scratch_shapes=[pltpu.VMEM((kb * nr, tall), jnp.float32), pltpu.VMEM((ka * nc, narrow), jnp.float32)],
        compiler_params=limit,
    )(part, mask, *m, acx, ack)


def solution(mesh):
    nr, nc = mesh.shape["row"], mesh.shape["col"]

    def whole(amplitudes, integrals, occ_counts, vir_counts):
        pairs, kw = amplitudes.shape
        sizes = (nr, nc, pairs // nr, pairs // nc, kw // nc, kw // nr)
        placed = (P("row", "col"), P("row", "col"), P(), P())
        return jax.shard_map(
            functools.partial(per_device, sizes), mesh=mesh, in_specs=placed, out_specs=P("row", "col"), check_vma=False
        )(amplitudes, integrals, occ_counts, vir_counts)

    return whole
```

time: 37 us -> 31.9 us (0.86)
  waiting for transfers between devices: 13.5 us -> 4.25 us
  starting transfers between devices: 19.3 us -> 22.2 us
  local copies, waits for them, and re-layouts: 0.14 us -> 1.65 us
  other arithmetic: 1.01 us -> 0.12 us
  Pallas kernels: 2.51 us -> 3.09 us
    ppermute x14 -> x13, waiting for transfers between devices: 13.5 us -> 4.25 us  [send(): return lax.ppermute(value, ('row', 'col'), pairs)]
    ppermute x14 -> x13, starting transfers between devices: 19.3 us -> 22.2 us  [send(): return lax.ppermute(value, ('row', 'col'), pairs)]
    unnamed x15, local copies, waits for them, and re-layouts: 0.1 us -> 1.58 us
    concatenate x1, other arithmetic: 0.93 us -> 0.02 us  [per_device(): ay = send(jnp.concatenate(a[0::2], 0), moved(0, 1))]
    pallas_call x1 -> x2, Pallas kernels: 2.51 us -> 3.09 us  [the longest x1 1.8 us: per_device(): pl.pallas_call(functools.partial(direct, sizes), out_shape=(tile, tile),...]
  transfers between devices with their start and end apart: 14 -> 13, of which waited for: 6 -> 4; matrix products, arithmetic and copies ran while one was open for 3% -> 3% of each run, Pallas kernels for 0% -> 6%
where the time goes in v2:
time: 31.9 us; the launch traced here: 31.6 us
  starting transfers between devices  22.2 us (70%)
  waiting for transfers between devices  4.25 us (13%)
  Pallas kernels  3.09 us (10%)
  local copies, waits for them, and re-layouts  1.65 us (5%)
    ppermute x13, starting transfers between devices, send(): return lax.ppermute(value, ('row', 'col'), pairs)  22.2 us
    ppermute x13, waiting for transfers between devices, send(): return lax.ppermute(value, ('row', 'col'), pairs)  4.25 us
    pallas_call x1, Pallas kernels, per_device(): pl.pallas_call(functools.partial(direct, sizes), out_shape=(tile, tile),...  1.8 us
    unnamed x15, local copies, waits for them, and re-layouts  1.58 us
    pallas_call x1, Pallas kernels, per_device(): pl.pallas_call(functools.partial(mirrored, sizes), out_shape=tile, in_spe...  1.3 us
  transfers between devices with their start and end apart: 13, of which 4 were waited for; matrix products, arithmetic and copies ran while one was open for 3% of the time, Pallas kernels for 6%

profile of v2, /device:TPU:0, one launch (start us, length us, event | category | flops | bytes accessed | tf_op | source)
XLA Modules:
  0.0 31.6 jit_solution(17372025987491399674)
XLA Ops:
  0.0 3.0 %collective-permute-start = (f32[32,512]{1,0:T(8,128)}, f32[32,512]{1,0:T(8,128)S(1)}, u32[]{:S(2)}, u32[]{:S(2)}) collective-permute-start(f32[32,512]{1,0:T(8,128)} %bitcast.6), channel_id=1, source_target_pairs={{0,2},{1,3},{2,0},{3,1},{4,6},{5,7},{6,4},{7,5},{8,10},{9,11},{10,... | collective-permute-start | bytes 196616 | tf_op jit(solution)/shard_map/ppermute | solution.py:86
  3.0 2.6 %collective-permute-start.1 = (f32[32,512]{1,0:T(8,128)}, f32[32,512]{1,0:T(8,128)S(1)}, u32[]{:S(2)}, u32[]{:S(2)}) collective-permute-start(f32[32,512]{1,0:T(8,128)} %bitcast.7), channel_id=1, source_target_pairs={{0,4},{1,5},{2,6},{3,7},{4,0},{5,1},{6,2},{7,3},{8,12},{9,13},{10,... | collective-permute-start | bytes 196616 | tf_op jit(solution)/shard_map/ppermute | solution.py:86
  5.6 0.0 collective-permute-start.2
  5.6 1.5 %collective-permute-start.6 = (f32[64,256]{1,0:T(8,128)}, f32[64,256]{1,0:T(8,128)S(1)}, u32[]{:S(2)}, u32[]{:S(2)}) collective-permute-start(f32[64,256]{1,0:T(8,128)} %refs_10_.1), channel_id=1, source_target_pairs={{0,0},{1,1},{2,8},{3,9},{4,16},{5,17},{6,24},{7,25},{8,2},{9,3},{1... | collective-permute-start | bytes 196616 | tf_op jit(solution)/shard_map/ppermute | solution.py:86
  7.1 4.5 %collective-permute-start.7 = (f32[64,256]{1,0:T(8,128)}, f32[64,256]{1,0:T(8,128)S(1)}, u32[]{:S(2)}, u32[]{:S(2)}) collective-permute-start(f32[64,256]{1,0:T(8,128)} %refs_10_.1), channel_id=1, source_target_pairs={{0,4},{1,5},{2,12},{3,13},{4,20},{5,21},{6,28},{7,29},{8,6},{9,7},... | collective-permute-start | bytes 196616 | tf_op jit(solution)/shard_map/ppermute | solution.py:86
  11.6 0.0 copy-start
  11.6 0.8 %constant_dynamic-update-slice_fusion.3 = (f32[256,256]{1,0:T(8,128)S(1)}, f32[32,256]{1,0:T(8,128)S(1)}) fusion(f32[512,32]{0,1:T(8,128)} %param.4, s32[]{:T(128)S(6)} %select_n.17), kind=kLoop, calls=%fused_computation.16 | loop fusion | bytes 98308
  12.5 0.0 copy-done
  12.5 0.0 collective-permute-done.refs_4_
  12.5 0.0 collective-permute-done.1.refs_6_
  12.5 0.0 collective-permute-done.2.refs_8_
  12.6 1.6 %collective-permute-start.3 = (f32[128,512]{1,0:T(8,128)S(1)}, f32[128,512]{1,0:T(8,128)S(1)}, u32[]{:S(2)}, u32[]{:S(2)}) collective-permute-start(f32[128,512]{1,0:T(8,128)S(1)} %pad_maximum_fusion), channel_id=1, source_target_pairs={{0,1},{1,0},{2,3},{3,2},{4,5},{5,4},{6,7},{7,6},{8,9},{9,8},{10,11... | collective-permute-start | bytes 786440 | tf_op jit(solution)/shard_map/ppermute | solution.py:86
  14.2 0.0 copy-start.1
  14.2 2.8 %collective-permute-start.10 = (f32[128,256]{1,0:T(8,128)S(1)}, f32[128,256]{1,0:T(8,128)S(1)}, u32[]{:S(2)}, u32[]{:S(2)}) collective-permute-start(f32[128,256]{1,0:T(8,128)S(1)} %pad_maximum_fusion.4), channel_id=1, source_target_pairs={{0,16},{1,17},{10,26},{11,27},{20,4},{21,5},{30,14},{31,15}} | collective-permute-start | bytes 393224 | tf_op jit(solution)/shard_map/ppermute | solution.py:86
  17.0 0.0 copy-done.1
  17.0 0.1 collective-permute-start.4
  17.1 0.0 collective-permute-done.6.refs_2_
  17.1 0.0 collective-permute-done.7.refs_6_
  17.1 0.1 collective-permute-start.8
  17.2 3.8 %collective-permute-start.11 = (f32[128,256]{1,0:T(8,128)S(1)}, f32[128,256]{1,0:T(8,128)S(1)}, u32[]{:S(2)}, u32[]{:S(2)}) collective-permute-start(f32[128,256]{1,0:T(8,128)S(1)} %pad_maximum_fusion.5), channel_id=1, source_target_pairs={{0,17},{1,16},{10,27},{11,26},{20,5},{21,4},{30,15},{31,14}} | collective-permute-start | bytes 393224 | tf_op jit(solution)/shard_map/ppermute | solution.py:86
  21.1 0.3 collective-permute-done.4.refs_12_
  21.4 0.1 collective-permute-start.5
  21.5 0.7 %collective-permute-done.8 = f32[128,256]{1,0:T(8,128)S(1)} collective-permute-done((f32[128,256]{1,0:T(8,128)S(1)}, f32[128,256]{1,0:T(8,128)S(1)}, u32[]{:S(2)}, u32[]{:S(2)}) %collective-permute-start.8) | collective-permute-done | bytes 131104 | tf_op jit(solution)/shard_map/ppermute | solution.py:86
  22.2 0.6 %collective-permute-start.9 = (f32[256,256]{1,0:T(8,128)S(1)}, f32[256,256]{1,0:T(8,128)S(1)}, u32[]{:S(2)}, u32[]{:S(2)}) collective-permute-start(f32[256,256]{1,0:T(8,128)S(1)} %pad_maximum_fusion.1), channel_id=1, source_target_pairs={{0,1},{1,0},{2,3},{3,2},{4,5},{5,4},{6,7},{7,6},{8,9},{9,8},{10,11... | collective-permute-start | bytes 786440 | tf_op jit(solution)/shard_map/ppermute | solution.py:86
  22.9 0.0 collective-permute-done.3
  23.0 0.0 collective-permute-done.10
  23.0 0.6 %collective-permute-done.11 = f32[128,256]{1,0:T(8,128)S(1)} collective-permute-done((f32[128,256]{1,0:T(8,128)S(1)}, f32[128,256]{1,0:T(8,128)S(1)}, u32[]{:S(2)}, u32[]{:S(2)}) %collective-permute-start.11) | collective-permute-done | bytes 131104 | tf_op jit(solution)/shard_map/ppermute | solution.py:86
  23.6 1.5 %collective-permute-start.12 = (f32[256,256]{1,0:T(8,128)S(1)}, f32[256,256]{1,0:T(8,128)S(1)}, u32[]{:S(2)}, u32[]{:S(2)}) collective-permute-start(f32[256,256]{1,0:T(8,128)S(1)} %maximum_select_fusion.refs_10_), channel_id=1, source_target_pairs={{0,8},{1,9},{4,12},{5,13},{10,2},{11,3},{14,6},{15,7},{16,24},{17,... | collective-permute-start | bytes 786440 | tf_op jit(solution)/shard_map/ppermute | solution.py:86
  25.2 0.0 collective-permute-done.5
  25.2 0.0 copy-start.2
  25.2 0.0 copy-start.3
  25.2 0.6 %copy-done.2 = s32[8]{0:T(128)S(1)} copy-done((s32[8]{0:T(128)S(1)}, s32[8]{0:T(128)}, u32[]{:S(2)}) %copy-start.2) | copy-done | bytes 56
  25.8 0.0 copy-done.3
  25.9 1.8 %shard_map.46 = (f32[512,256]{1,0:T(8,128)S(1)}, f32[512,256]{1,0:T(8,128)S(1)}) custom-call(s32[8]{0:T(128)S(1)} %copy-done.2, s32[8]{0:T(128)S(1)} %copy-done.3, f32[32,512]{1,0:T(8,128)S(1)} %bitcast.10, f32[32,512]{1,0:T(8,128)S(1)} %get-tuple-element.28.refs_3_, f32[32,512]{1,0:T(8,128)S(1)} %collective-permute-done.refs_4_, ...), custom_call_target="tpu_custom_call" | custom-call | tf_op jit(solution)/shard_map/pallas_call | solution.py:141
  27.7 2.6 %collective-permute-done.9 = f32[256,256]{1,0:T(8,128)S(1)} collective-permute-done((f32[256,256]{1,0:T(8,128)S(1)}, f32[256,256]{1,0:T(8,128)S(1)}, u32[]{:S(2)}, u32[]{:S(2)}) %collective-permute-start.9) | collective-permute-done | bytes 262176 | tf_op jit(solution)/shard_map/ppermute | solution.py:86
  30.3 0.0 collective-permute-done.12.refs_11_
  30.3 1.3 %shard_map.47 = f32[512,256]{1,0:T(8,128)} custom-call(f32[512,256]{1,0:T(8,128)S(1)} %get-tuple-element.10.refs_0_, f32[512,256]{1,0:T(8,128)S(1)} %get-tuple-element.11.refs_1_, f32[64,256]{1,0:T(8,128)S(1)} %collective-permute-done.6.refs_2_, f32[64,256]{1,0:T(8,128)S(1)} %get-tuple-element.24.refs_3_, f32[64,256]{1,0:T(8,128)S(1)} %get-tuple-element.29.refs_4_, ...), custom_call_target="tpu_custom_call" | custom-call | tf_op jit(solution)/shard_map/pallas_call | solution.py:149
  (19 shorter events, 0.3 us)
Async XLA Ops:
  0.0 12.5 %collective-permute-start = (f32[32,512]{1,0:T(8,128)}, f32[32,512]{1,0:T(8,128)S(1)}, u32[]{:S(2)}, u32[]{:S(2)}) collective-permute-start(f32[32,512]{1,0:T(8,128)} %bitcast.6), channel_id=1, source_target_pairs={{0,2},{1,3},{2,0},{3,1},{4,6},{5,7},{6,4},{7,5},{8,10},{9,11},{10,... | collective-permute-start | bytes 196616 | tf_op jit(solution)/shard_map/ppermute | solution.py:86
  3.0 9.5 %collective-permute-start.1 = (f32[32,512]{1,0:T(8,128)}, f32[32,512]{1,0:T(8,128)S(1)}, u32[]{:S(2)}, u32[]{:S(2)}) collective-permute-start(f32[32,512]{1,0:T(8,128)} %bitcast.7), channel_id=1, source_target_pairs={{0,4},{1,5},{2,6},{3,7},{4,0},{5,1},{6,2},{7,3},{8,12},{9,13},{10,... | collective-permute-start | bytes 196616 | tf_op jit(solution)/shard_map/ppermute | solution.py:86
  5.6 6.9 %collective-permute-start.2 = (f32[32,512]{1,0:T(8,128)}, f32[32,512]{1,0:T(8,128)S(1)}, u32[]{:S(2)}, u32[]{:S(2)}) collective-permute-start(f32[32,512]{1,0:T(8,128)} %bitcast.8), channel_id=1, source_target_pairs={{0,6},{1,7},{2,4},{3,5},{4,2},{5,3},{6,0},{7,1},{8,14},{9,15},{10,... | collective-permute-start | bytes 196616 | tf_op jit(solution)/shard_map/ppermute | solution.py:86
  5.6 11.5 %collective-permute-start.6 = (f32[64,256]{1,0:T(8,128)}, f32[64,256]{1,0:T(8,128)S(1)}, u32[]{:S(2)}, u32[]{:S(2)}) collective-permute-start(f32[64,256]{1,0:T(8,128)} %refs_10_.1), channel_id=1, source_target_pairs={{0,0},{1,1},{2,8},{3,9},{4,16},{5,17},{6,24},{7,25},{8,2},{9,3},{1... | collective-permute-start | bytes 196616 | tf_op jit(solution)/shard_map/ppermute | solution.py:86
  7.1 10.0 %collective-permute-start.7 = (f32[64,256]{1,0:T(8,128)}, f32[64,256]{1,0:T(8,128)S(1)}, u32[]{:S(2)}, u32[]{:S(2)}) collective-permute-start(f32[64,256]{1,0:T(8,128)} %refs_10_.1), channel_id=1, source_target_pairs={{0,4},{1,5},{2,12},{3,13},{4,20},{5,21},{6,28},{7,29},{8,6},{9,7},... | collective-permute-start | bytes 196616 | tf_op jit(solution)/shard_map/ppermute | solution.py:86
  11.6 0.8 %copy-start = (f32[512,32]{0,1:T(8,128)S(1)}, f32[512,32]{0,1:T(8,128)}, u32[]{:S(2)}) copy-start(f32[512,32]{0,1:T(8,128)} %param.4) | copy-start | bytes 196612
  12.6 10.3 %collective-permute-start.3 = (f32[128,512]{1,0:T(8,128)S(1)}, f32[128,512]{1,0:T(8,128)S(1)}, u32[]{:S(2)}, u32[]{:S(2)}) collective-permute-start(f32[128,512]{1,0:T(8,128)S(1)} %pad_maximum_fusion), channel_id=1, source_target_pairs={{0,1},{1,0},{2,3},{3,2},{4,5},{5,4},{6,7},{7,6},{8,9},{9,8},{10,11... | collective-permute-start | bytes 786440 | tf_op jit(solution)/shard_map/ppermute | solution.py:86
  14.2 2.8 %copy-start.1 = (f32[64,256]{1,0:T(8,128)S(1)}, f32[64,256]{1,0:T(8,128)}, u32[]{:S(2)}) copy-start(f32[64,256]{1,0:T(8,128)} %refs_10_.1) | copy-start | bytes 196612
  14.2 8.7 %collective-permute-start.10 = (f32[128,256]{1,0:T(8,128)S(1)}, f32[128,256]{1,0:T(8,128)S(1)}, u32[]{:S(2)}, u32[]{:S(2)}) collective-permute-start(f32[128,256]{1,0:T(8,128)S(1)} %pad_maximum_fusion.4), channel_id=1, source_target_pairs={{0,16},{1,17},{10,26},{11,27},{20,4},{21,5},{30,14},{31,15}} | collective-permute-start | bytes 393224 | tf_op jit(solution)/shard_map/ppermute | solution.py:86
  17.0 4.3 %collective-permute-start.4 = (f32[64,256]{1,0:T(8,128)S(1)}, f32[64,256]{1,0:T(8,128)S(1)}, u32[]{:S(2)}, u32[]{:S(2)}) collective-permute-start(f32[64,256]{1,0:T(8,128)S(1)} %copy-done.1), channel_id=1, source_target_pairs={{0,16},{1,17},{2,18},{3,19},{4,20},{5,21},{6,22},{7,23},{8,24},{9,... | collective-permute-start | bytes 196616 | tf_op jit(solution)/shard_map/ppermute | solution.py:86
  17.1 5.0 %collective-permute-start.8 = (f32[128,256]{1,0:T(8,128)S(1)}, f32[128,256]{1,0:T(8,128)S(1)}, u32[]{:S(2)}, u32[]{:S(2)}) collective-permute-start(f32[128,256]{1,0:T(8,128)S(1)} %pad_maximum_fusion.3), channel_id=1, source_target_pairs={{0,2},{1,3},{2,0},{3,1},{4,6},{5,7},{6,4},{7,5},{8,10},{9,11},{10,... | collective-permute-start | bytes 393224 | tf_op jit(solution)/shard_map/ppermute | solution.py:86
  17.2 6.4 %collective-permute-start.11 = (f32[128,256]{1,0:T(8,128)S(1)}, f32[128,256]{1,0:T(8,128)S(1)}, u32[]{:S(2)}, u32[]{:S(2)}) collective-permute-start(f32[128,256]{1,0:T(8,128)S(1)} %pad_maximum_fusion.5), channel_id=1, source_target_pairs={{0,17},{1,16},{10,27},{11,26},{20,5},{21,4},{30,15},{31,14}} | collective-permute-start | bytes 393224 | tf_op jit(solution)/shard_map/ppermute | solution.py:86
  21.4 3.8 %collective-permute-start.5 = (f32[128,256]{1,0:T(8,128)S(1)}, f32[128,256]{1,0:T(8,128)S(1)}, u32[]{:S(2)}, u32[]{:S(2)}) collective-permute-start(f32[128,256]{1,0:T(8,128)S(1)} %pad_maximum_fusion.2), channel_id=1, source_target_pairs={{0,8},{1,9},{2,10},{3,11},{4,12},{5,13},{6,14},{7,15},{8,0},{9,1},... | collective-permute-start | bytes 393224 | tf_op jit(solution)/shard_map/ppermute | solution.py:86
  22.2 8.0 %collective-permute-start.9 = (f32[256,256]{1,0:T(8,128)S(1)}, f32[256,256]{1,0:T(8,128)S(1)}, u32[]{:S(2)}, u32[]{:S(2)}) collective-permute-start(f32[256,256]{1,0:T(8,128)S(1)} %pad_maximum_fusion.1), channel_id=1, source_target_pairs={{0,1},{1,0},{2,3},{3,2},{4,5},{5,4},{6,7},{7,6},{8,9},{9,8},{10,11... | collective-permute-start | bytes 786440 | tf_op jit(solution)/shard_map/ppermute | solution.py:86
  23.6 6.7 %collective-permute-start.12 = (f32[256,256]{1,0:T(8,128)S(1)}, f32[256,256]{1,0:T(8,128)S(1)}, u32[]{:S(2)}, u32[]{:S(2)}) collective-permute-start(f32[256,256]{1,0:T(8,128)S(1)} %maximum_select_fusion.refs_10_), channel_id=1, source_target_pairs={{0,8},{1,9},{4,12},{5,13},{10,2},{11,3},{14,6},{15,7},{16,24},{17,... | collective-permute-start | bytes 786440 | tf_op jit(solution)/shard_map/ppermute | solution.py:86
  25.2 0.7 %copy-start.2 = (s32[8]{0:T(128)S(1)}, s32[8]{0:T(128)}, u32[]{:S(2)}) copy-start(s32[8]{0:T(128)} %refs_0_.1) | copy-start | bytes 100
  25.2 0.7 %copy-start.3 = (s32[8]{0:T(128)S(1)}, s32[8]{0:T(128)}, u32[]{:S(2)}) copy-start(s32[8]{0:T(128)} %refs_1_.1) | copy-start | bytes 100

commit v3 on v2

--- a/solution.py
+++ b/solution.py
@@ -109,24 +109,22 @@
     m = [None] * nc
     b = [None] * nr
     b[0] = integrals
+    b[1] = send(integrals, moved(1, 0))
+    pair = jnp.concatenate([integrals, b[1]], axis=0)
     for d in range(nz - 1, 0, -1):
         a[2 * d] = send(at, moved(0, 2 * d))
     for e in range(0, nz, 2):
-        m[2 * e] = send(integrals, mirror(e))
+        got = send(pair, mirror(e))
+        m[2 * e], m[2 * e + 2] = got[:kb], got[kb:]
     for d in range(2, nr, 2):
-        b[d] = send(after(integrals, *a[2::2]), moved(d, 0))
+        got = send(after(pair, *a[2::2]), moved(d, 0))
+        b[d], b[d + 1] = got[:kb], got[kb:]
     ay = send(jnp.concatenate(a[0::2], 0), moved(0, 1))
     for d in range(nz):
         a[2 * d + 1] = ay[d * ka : (d + 1) * ka]
-    mz = send(jnp.concatenate(m[0::4], 0), moved(0, 2))
-    for i in range(nz // 2):
-        m[4 * i + 2] = mz[i * kb : (i + 1) * kb]
-    bk = send(jnp.concatenate(b[0::2], 0), moved(1, 0))
-    for d in range(0, nr, 2):
-        b[d + 1] = bk[d // 2 * kb : (d // 2 + 1) * kb]
     px = half_of(a[0::2], y)
     px = sum(send(px, moved(d, 0, home)) for d in range(2, nr, 2))
-    pxy = after(half_of(a[0::2], 1 - y), *a[2::2])
+    pxy = half_of(a[0::2], 1 - y)
     pxy = sum(send(pxy, moved(d, 1, home)) for d in range(2, nr, 2))
     my = send(jnp.concatenate(m[0::2], 0), moved(0, 1))
     for d in range(nz):

time: 31.9 us -> 29.4 us (0.922)
  waiting for transfers between devices: 4.25 us -> 1.88 us
    ppermute x13 -> x12, waiting for transfers between devices: 4.25 us -> 1.88 us  [send(): return lax.ppermute(value, ('row', 'col'), pairs)]
    ppermute x13 -> x12, starting transfers between devices: 22.2 us -> 22.1 us  [send(): return lax.ppermute(value, ('row', 'col'), pairs)]
    unnamed x15 -> x16, local copies, waits for them, and re-layouts: 1.58 us -> 1.63 us
  transfers between devices with their start and end apart: 13 -> 12, of which waited for: 4 -> 3; matrix products, arithmetic and copies ran while one was open for 3% -> 4% of each run, Pallas kernels for 6% -> 6%
where the time goes in v3:
time: 29.4 us; the launch traced here: 29.2 us
  starting transfers between devices  22.1 us (75%)
  Pallas kernels  3.09 us (11%)
  waiting for transfers between devices  1.88 us (6%)
  local copies, waits for them, and re-layouts  1.73 us (6%)
    ppermute x12, starting transfers between devices, send(): return lax.ppermute(value, ('row', 'col'), pairs)  22.1 us
    ppermute x12, waiting for transfers between devices, send(): return lax.ppermute(value, ('row', 'col'), pairs)  1.88 us
    pallas_call x1, Pallas kernels, per_device(): pl.pallas_call(functools.partial(direct, sizes), out_shape=(tile, tile),...  1.79 us
    unnamed x16, local copies, waits for them, and re-layouts  1.63 us
    pallas_call x1, Pallas kernels, per_device(): pl.pallas_call(functools.partial(mirrored, sizes), out_shape=tile, in_spe...  1.3 us
  transfers between devices with their start and end apart: 12, of which 3 were waited for; matrix products, arithmetic and copies ran while one was open for 4% of the time, Pallas kernels for 6%

profile of v3, /device:TPU:0, one launch (start us, length us, event | category | flops | bytes accessed | tf_op | source)
XLA Modules:
  0.0 29.2 jit_solution(3728396644041808965)
XLA Ops:
  0.0 3.0 %collective-permute-start = (f32[32,512]{1,0:T(8,128)}, f32[32,512]{1,0:T(8,128)S(1)}, u32[]{:S(2)}, u32[]{:S(2)}) collective-permute-start(f32[32,512]{1,0:T(8,128)} %bitcast.6), channel_id=1, source_target_pairs={{0,2},{1,3},{2,0},{3,1},{4,6},{5,7},{6,4},{7,5},{8,10},{9,11},{10,... | collective-permute-start | bytes 196616 | tf_op jit(solution)/shard_map/ppermute | solution.py:86
  3.0 2.6 %collective-permute-start.1 = (f32[32,512]{1,0:T(8,128)}, f32[32,512]{1,0:T(8,128)S(1)}, u32[]{:S(2)}, u32[]{:S(2)}) collective-permute-start(f32[32,512]{1,0:T(8,128)} %bitcast.7), channel_id=1, source_target_pairs={{0,4},{1,5},{2,6},{3,7},{4,0},{5,1},{6,2},{7,3},{8,12},{9,13},{10,... | collective-permute-start | bytes 196616 | tf_op jit(solution)/shard_map/ppermute | solution.py:86
  5.6 0.0 collective-permute-start.2
  5.6 0.0 collective-permute-start.4
  5.6 0.0 copy-start
  5.6 0.9 %constant_dynamic-update-slice_fusion.1 = f32[128,256]{1,0:T(8,128)S(1)} fusion(f32[64,256]{1,0:T(8,128)} %refs_10_.1), kind=kLoop, calls=%fused_computation.12 | loop fusion | bytes 131072
  6.5 0.0 copy-done
  6.6 0.5 %collective-permute-done.4.refs_11_ = f32[64,256]{1,0:T(8,128)S(1)} collective-permute-done((f32[64,256]{1,0:T(8,128)}, f32[64,256]{1,0:T(8,128)S(1)}, u32[]{:S(2)}, u32[]{:S(2)}) %collective-permute-start.4) | collective-permute-done | bytes 65568 | tf_op jit(solution)/shard_map/ppermute | solution.py:86
  7.1 0.7 %collective-permute-start.6 = (f32[128,256]{1,0:T(8,128)S(1)}, f32[128,256]{1,0:T(8,128)S(1)}, u32[]{:S(2)}, u32[]{:S(2)}) collective-permute-start(f32[128,256]{1,0:T(8,128)S(1)} %constant_dynamic-update-slice_fusion), channel_id=1, source_target_pairs={{0,0},{1,1},{2,8},{3,9},{4,16},{5,17},{6,24},{7,25},{8,2},{9,3},{1... | collective-permute-start | bytes 393224 | tf_op jit(solution)/shard_map/ppermute | solution.py:86
  7.8 5.4 %collective-permute-start.7 = (f32[128,256]{1,0:T(8,128)S(1)}, f32[128,256]{1,0:T(8,128)S(1)}, u32[]{:S(2)}, u32[]{:S(2)}) collective-permute-start(f32[128,256]{1,0:T(8,128)S(1)} %constant_dynamic-update-slice_fusion), channel_id=1, source_target_pairs={{0,4},{1,5},{2,12},{3,13},{4,20},{5,21},{6,28},{7,29},{8,6},{9,7},... | collective-permute-start | bytes 393224 | tf_op jit(solution)/shard_map/ppermute | solution.py:86
  13.1 0.0 collective-permute-done.refs_4_
  13.1 0.0 collective-permute-done.1.refs_6_
  13.1 0.0 collective-permute-done.2.refs_8_
  13.2 1.6 %collective-permute-start.3 = (f32[128,512]{1,0:T(8,128)S(1)}, f32[128,512]{1,0:T(8,128)S(1)}, u32[]{:S(2)}, u32[]{:S(2)}) collective-permute-start(f32[128,512]{1,0:T(8,128)S(1)} %pad_maximum_fusion), channel_id=1, source_target_pairs={{0,1},{1,0},{2,3},{3,2},{4,5},{5,4},{6,7},{7,6},{8,9},{9,8},{10,11... | collective-permute-start | bytes 786440 | tf_op jit(solution)/shard_map/ppermute | solution.py:86
  14.8 2.2 %collective-permute-start.9 = (f32[128,256]{1,0:T(8,128)S(1)}, f32[128,256]{1,0:T(8,128)S(1)}, u32[]{:S(2)}, u32[]{:S(2)}) collective-permute-start(f32[128,256]{1,0:T(8,128)S(1)} %pad_maximum_fusion.2), channel_id=1, source_target_pairs={{0,16},{1,17},{10,26},{11,27},{20,4},{21,5},{30,14},{31,15}} | collective-permute-start | bytes 393224 | tf_op jit(solution)/shard_map/ppermute | solution.py:86
  17.0 1.3 %collective-permute-start.10 = (f32[128,256]{1,0:T(8,128)S(1)}, f32[128,256]{1,0:T(8,128)S(1)}, u32[]{:S(2)}, u32[]{:S(2)}) collective-permute-start(f32[128,256]{1,0:T(8,128)S(1)} %pad_maximum_fusion.3), channel_id=1, source_target_pairs={{0,17},{1,16},{10,27},{11,26},{20,5},{21,4},{30,15},{31,14}} | collective-permute-start | bytes 393224 | tf_op jit(solution)/shard_map/ppermute | solution.py:86
  18.3 0.0 collective-permute-done.6
  18.3 2.0 %collective-permute-start.5 = (f32[128,256]{1,0:T(8,128)S(1)}, f32[128,256]{1,0:T(8,128)S(1)}, u32[]{:S(2)}, u32[]{:S(2)}) collective-permute-start(f32[128,256]{1,0:T(8,128)S(1)} %constant_dynamic-update-slice_fusion), channel_id=1, source_target_pairs={{0,16},{1,17},{2,18},{3,19},{4,20},{5,21},{6,22},{7,23},{8,24},{9,... | collective-permute-start | bytes 393224 | tf_op jit(solution)/shard_map/ppermute | solution.py:86
  20.3 0.0 collective-permute-done.7
  20.3 1.7 %collective-permute-start.8 = (f32[256,256]{1,0:T(8,128)S(1)}, f32[256,256]{1,0:T(8,128)S(1)}, u32[]{:S(2)}, u32[]{:S(2)}) collective-permute-start(f32[256,256]{1,0:T(8,128)S(1)} %pad_maximum_fusion.1), channel_id=1, source_target_pairs={{0,1},{1,0},{2,3},{3,2},{4,5},{5,4},{6,7},{7,6},{8,9},{9,8},{10,11... | collective-permute-start | bytes 786440 | tf_op jit(solution)/shard_map/ppermute | solution.py:86
  22.0 0.4 %collective-permute-done.3 = f32[128,512]{1,0:T(8,128)S(1)} collective-permute-done((f32[128,512]{1,0:T(8,128)S(1)}, f32[128,512]{1,0:T(8,128)S(1)}, u32[]{:S(2)}, u32[]{:S(2)}) %collective-permute-start.3) | collective-permute-done | bytes 262176 | tf_op jit(solution)/shard_map/ppermute | solution.py:86
  22.5 0.0 collective-permute-done.9
  22.5 0.0 collective-permute-done.10
  22.6 0.0 copy-start.1
  22.6 1.8 %collective-permute-start.11 = (f32[256,256]{1,0:T(8,128)S(1)}, f32[256,256]{1,0:T(8,128)S(1)}, u32[]{:S(2)}, u32[]{:S(2)}) collective-permute-start(f32[256,256]{1,0:T(8,128)S(1)} %maximum_select_fusion.refs_10_), channel_id=1, source_target_pairs={{0,8},{1,9},{4,12},{5,13},{10,2},{11,3},{14,6},{15,7},{16,24},{17,... | collective-permute-start | bytes 786440 | tf_op jit(solution)/shard_map/ppermute | solution.py:86
  24.4 0.0 collective-permute-done.5
  24.4 0.0 copy-start.2
  24.4 0.0 copy-start.3
  24.4 0.0 copy-done.1
  24.4 0.6 %copy-done.2 = s32[8]{0:T(128)S(1)} copy-done((s32[8]{0:T(128)S(1)}, s32[8]{0:T(128)}, u32[]{:S(2)}) %copy-start.2) | copy-done | bytes 56
  25.1 0.0 copy-done.3
  25.1 1.8 %shard_map.46 = (f32[512,256]{1,0:T(8,128)S(1)}, f32[512,256]{1,0:T(8,128)S(1)}) custom-call(s32[8]{0:T(128)S(1)} %copy-done.2, s32[8]{0:T(128)S(1)} %copy-done.3, f32[32,512]{1,0:T(8,128)S(1)} %bitcast.10, f32[32,512]{1,0:T(8,128)S(1)} %get-tuple-element.26.refs_3_, f32[32,512]{1,0:T(8,128)S(1)} %collective-permute-done.refs_4_, ...), custom_call_target="tpu_custom_call" | custom-call | tf_op jit(solution)/shard_map/pallas_call | solution.py:139
  26.9 1.0 %collective-permute-done.8 = f32[256,256]{1,0:T(8,128)S(1)} collective-permute-done((f32[256,256]{1,0:T(8,128)S(1)}, f32[256,256]{1,0:T(8,128)S(1)}, u32[]{:S(2)}, u32[]{:S(2)}) %collective-permute-start.8) | collective-permute-done | bytes 262176 | tf_op jit(solution)/shard_map/ppermute | solution.py:86
  27.9 0.0 collective-permute-done.11.refs_11_
  27.9 1.3 %shard_map.47 = f32[512,256]{1,0:T(8,128)} custom-call(f32[512,256]{1,0:T(8,128)S(1)} %get-tuple-element.9.refs_0_, f32[512,256]{1,0:T(8,128)S(1)} %get-tuple-element.10.refs_1_, f32[64,256]{1,0:T(8,128)S(1)} %get-tuple-element.30.refs_2_, f32[64,256]{1,0:T(8,128)S(1)} %get-tuple-element.22.refs_3_, f32[64,256]{1,0:T(8,128)S(1)} %get-tuple-element.29.refs_4_, ...), custom_call_target="tpu_custom_call" | custom-call | tf_op jit(solution)/shard_map/pallas_call | solution.py:147
  (20 shorter events, 0.3 us)
Async XLA Ops:
  0.0 13.1 %collective-permute-start = (f32[32,512]{1,0:T(8,128)}, f32[32,512]{1,0:T(8,128)S(1)}, u32[]{:S(2)}, u32[]{:S(2)}) collective-permute-start(f32[32,512]{1,0:T(8,128)} %bitcast.6), channel_id=1, source_target_pairs={{0,2},{1,3},{2,0},{3,1},{4,6},{5,7},{6,4},{7,5},{8,10},{9,11},{10,... | collective-permute-start | bytes 196616 | tf_op jit(solution)/shard_map/ppermute | solution.py:86
  3.0 10.1 %collective-permute-start.1 = (f32[32,512]{1,0:T(8,128)}, f32[32,512]{1,0:T(8,128)S(1)}, u32[]{:S(2)}, u32[]{:S(2)}) collective-permute-start(f32[32,512]{1,0:T(8,128)} %bitcast.7), channel_id=1, source_target_pairs={{0,4},{1,5},{2,6},{3,7},{4,0},{5,1},{6,2},{7,3},{8,12},{9,13},{10,... | collective-permute-start | bytes 196616 | tf_op jit(solution)/shard_map/ppermute | solution.py:86
  5.6 7.5 %collective-permute-start.2 = (f32[32,512]{1,0:T(8,128)}, f32[32,512]{1,0:T(8,128)S(1)}, u32[]{:S(2)}, u32[]{:S(2)}) collective-permute-start(f32[32,512]{1,0:T(8,128)} %bitcast.8), channel_id=1, source_target_pairs={{0,6},{1,7},{2,4},{3,5},{4,2},{5,3},{6,0},{7,1},{8,14},{9,15},{10,... | collective-permute-start | bytes 196616 | tf_op jit(solution)/shard_map/ppermute | solution.py:86
  5.6 1.5 %collective-permute-start.4 = (f32[64,256]{1,0:T(8,128)}, f32[64,256]{1,0:T(8,128)S(1)}, u32[]{:S(2)}, u32[]{:S(2)}) collective-permute-start(f32[64,256]{1,0:T(8,128)} %refs_10_.1), channel_id=1, source_target_pairs={{0,8},{1,9},{2,10},{3,11},{4,12},{5,13},{6,14},{7,15},{8,0},{9,1},... | collective-permute-start | bytes 196616 | tf_op jit(solution)/shard_map/ppermute | solution.py:86
  5.6 0.9 %copy-start = (f32[512,32]{0,1:T(8,128)S(1)}, f32[512,32]{0,1:T(8,128)}, u32[]{:S(2)}) copy-start(f32[512,32]{0,1:T(8,128)} %param.4) | copy-start | bytes 196612
  7.1 11.2 %collective-permute-start.6 = (f32[128,256]{1,0:T(8,128)S(1)}, f32[128,256]{1,0:T(8,128)S(1)}, u32[]{:S(2)}, u32[]{:S(2)}) collective-permute-start(f32[128,256]{1,0:T(8,128)S(1)} %constant_dynamic-update-slice_fusion), channel_id=1, source_target_pairs={{0,0},{1,1},{2,8},{3,9},{4,16},{5,17},{6,24},{7,25},{8,2},{9,3},{1... | collective-permute-start | bytes 393224 | tf_op jit(solution)/shard_map/ppermute | solution.py:86
  7.8 12.6 %collective-permute-start.7 = (f32[128,256]{1,0:T(8,128)S(1)}, f32[128,256]{1,0:T(8,128)S(1)}, u32[]{:S(2)}, u32[]{:S(2)}) collective-permute-start(f32[128,256]{1,0:T(8,128)S(1)} %constant_dynamic-update-slice_fusion), channel_id=1, source_target_pairs={{0,4},{1,5},{2,12},{3,13},{4,20},{5,21},{6,28},{7,29},{8,6},{9,7},... | collective-permute-start | bytes 393224 | tf_op jit(solution)/shard_map/ppermute | solution.py:86
  13.2 9.2 %collective-permute-start.3 = (f32[128,512]{1,0:T(8,128)S(1)}, f32[128,512]{1,0:T(8,128)S(1)}, u32[]{:S(2)}, u32[]{:S(2)}) collective-permute-start(f32[128,512]{1,0:T(8,128)S(1)} %pad_maximum_fusion), channel_id=1, source_target_pairs={{0,1},{1,0},{2,3},{3,2},{4,5},{5,4},{6,7},{7,6},{8,9},{9,8},{10,11... | collective-permute-start | bytes 786440 | tf_op jit(solution)/shard_map/ppermute | solution.py:86
  14.8 7.7 %collective-permute-start.9 = (f32[128,256]{1,0:T(8,128)S(1)}, f32[128,256]{1,0:T(8,128)S(1)}, u32[]{:S(2)}, u32[]{:S(2)}) collective-permute-start(f32[128,256]{1,0:T(8,128)S(1)} %pad_maximum_fusion.2), channel_id=1, source_target_pairs={{0,16},{1,17},{10,26},{11,27},{20,4},{21,5},{30,14},{31,15}} | collective-permute-start | bytes 393224 | tf_op jit(solution)/shard_map/ppermute | solution.py:86
  17.0 5.5 %collective-permute-start.10 = (f32[128,256]{1,0:T(8,128)S(1)}, f32[128,256]{1,0:T(8,128)S(1)}, u32[]{:S(2)}, u32[]{:S(2)}) collective-permute-start(f32[128,256]{1,0:T(8,128)S(1)} %pad_maximum_fusion.3), channel_id=1, source_target_pairs={{0,17},{1,16},{10,27},{11,26},{20,5},{21,4},{30,15},{31,14}} | collective-permute-start | bytes 393224 | tf_op jit(solution)/shard_map/ppermute | solution.py:86
  18.3 6.0 %collective-permute-start.5 = (f32[128,256]{1,0:T(8,128)S(1)}, f32[128,256]{1,0:T(8,128)S(1)}, u32[]{:S(2)}, u32[]{:S(2)}) collective-permute-start(f32[128,256]{1,0:T(8,128)S(1)} %constant_dynamic-update-slice_fusion), channel_id=1, source_target_pairs={{0,16},{1,17},{2,18},{3,19},{4,20},{5,21},{6,22},{7,23},{8,24},{9,... | collective-permute-start | bytes 393224 | tf_op jit(solution)/shard_map/ppermute | solution.py:86
  20.3 7.5 %collective-permute-start.8 = (f32[256,256]{1,0:T(8,128)S(1)}, f32[256,256]{1,0:T(8,128)S(1)}, u32[]{:S(2)}, u32[]{:S(2)}) collective-permute-start(f32[256,256]{1,0:T(8,128)S(1)} %pad_maximum_fusion.1), channel_id=1, source_target_pairs={{0,1},{1,0},{2,3},{3,2},{4,5},{5,4},{6,7},{7,6},{8,9},{9,8},{10,11... | collective-permute-start | bytes 786440 | tf_op jit(solution)/shard_map/ppermute | solution.py:86
  22.6 1.9 %copy-start.1 = (f32[64,256]{1,0:T(8,128)S(1)}, f32[64,256]{1,0:T(8,128)}, u32[]{:S(2)}) copy-start(f32[64,256]{1,0:T(8,128)} %refs_10_.1) | copy-start | bytes 196612
  22.6 5.3 %collective-permute-start.11 = (f32[256,256]{1,0:T(8,128)S(1)}, f32[256,256]{1,0:T(8,128)S(1)}, u32[]{:S(2)}, u32[]{:S(2)}) collective-permute-start(f32[256,256]{1,0:T(8,128)S(1)} %maximum_select_fusion.refs_10_), channel_id=1, source_target_pairs={{0,8},{1,9},{4,12},{5,13},{10,2},{11,3},{14,6},{15,7},{16,24},{17,... | collective-permute-start | bytes 786440 | tf_op jit(solution)/shard_map/ppermute | solution.py:86
  24.4 0.7 %copy-start.2 = (s32[8]{0:T(128)S(1)}, s32[8]{0:T(128)}, u32[]{:S(2)}) copy-start(s32[8]{0:T(128)} %refs_0_.1) | copy-start | bytes 100
  24.4 0.7 %copy-start.3 = (s32[8]{0:T(128)S(1)}, s32[8]{0:T(128)}, u32[]{:S(2)}) copy-start(s32[8]{0:T(128)} %refs_1_.1) | copy-start | bytes 100

commit v4 on v3

--- a/solution.py
+++ b/solution.py
@@ -35,17 +35,28 @@
     return mm(lh, rl) + mm(ll, rh) + mm(lh, rh)
 
 
+def twist(row, e):
+    return (row ^ (row >> 1) ^ 1) & 1 if e // 2 % 2 == 2 else 0
+
+
 def direct(sizes, *refs):
     nr, nc, tall, narrow, ka, kb = sizes
-    occ_ref, vir_ref = refs[:2]
     a_refs, b_refs = refs[2 : 2 + nc], refs[2 + nc : 2 + nc + nr]
-    out_ref, mask_ref, left, right = refs[2 + nc + nr :]
+    out_ref, mask_ref, left, right, occ_ref, vir_ref, sems = refs[2 + nc + nr :]
+    copies = [
+        pltpu.make_async_copy(refs[0], occ_ref, sems.at[0]),
+        pltpu.make_async_copy(refs[1], vir_ref, sems.at[1]),
+    ]
+    for copy in copies:
+        copy.start()
     row, col = lax.axis_index("row"), lax.axis_index("col")
     for d in range(nc):
         left[pl.ds(pl.multiple_of((col ^ d) * ka, ka), ka), :] = a_refs[d][...]
     for d in range(nr):
         right[pl.ds(pl.multiple_of((row ^ d) * kb, kb), kb), :] = b_refs[d][...]
     out_ref[...] = product(left[...], right[...])
+    for copy in copies:
+        copy.wait()
     occ, vir = [], []
     one = two = 0
     for h in range(IRREPS - 1):
@@ -65,13 +76,14 @@
     out_ref, left, right = refs[4 + nc :]
     col = lax.axis_index("col")
     z, y = col // 2, lax.rem(col, 2)
+    mine = lax.rem(lax.axis_index("row"), 2) == lax.rem(z, 2)
     for d in range(nc):
-        at = pl.multiple_of((z ^ (d // 2)) * kb, kb)
+        at = pl.multiple_of((z ^ (d // 2) ^ twist(lax.axis_index("row"), d // 2)) * kb, kb)
         lane = pl.multiple_of((y ^ (d % 2)) * narrow, narrow)
         left[pl.ds(at, kb), pl.ds(lane, narrow)] = m_refs[d][...]
         at = pl.multiple_of((col ^ d) * ka, ka)
         rows = pl.ds((d % 2 * nz + d // 2) * ka, ka)
-        right[pl.ds(at, ka), :] = ac_refs[0][rows, :] + ac_refs[1][rows, :]
+        right[pl.ds(at, ka), :] = jnp.where(mine, ac_refs[0][rows, :], ac_refs[1][rows, :])
     total = part_ref[...] + product(left[...], right[...])
     out_ref[...] = jnp.where(mask_ref[...] > 0.0, total, 0.0)
 
@@ -89,7 +101,7 @@
         return [(r * nc + c, (r ^ dr) * nc + (c ^ dc)) for r in range(nr) for c in range(nc) if keep(r, c)]
 
     def mirror(e):
-        return [(r * nc + c, (c // 2) * nc + 2 * (r ^ e) + c % 2) for r in range(nr) for c in range(nc)]
+        return [(r * nc + c, (c // 2) * nc + 2 * (r ^ e ^ twist(c // 2, e)) + c % 2) for r in range(nr) for c in range(nc)]
 
     def after(value, *others):
         return lax.optimization_barrier((value, *others))[0]
@@ -113,9 +125,9 @@
     pair = jnp.concatenate([integrals, b[1]], axis=0)
     for d in range(nz - 1, 0, -1):
         a[2 * d] = send(at, moved(0, 2 * d))
-    for e in range(0, nz, 2):
+    for e in [e ^ 1 ^ (e // 2 % 2) for e in range(0, nz, 2)]:
         got = send(pair, mirror(e))
-        m[2 * e], m[2 * e + 2] = got[:kb], got[kb:]
+        m[2 * e], m[2 * (e ^ 1)] = got[:kb], got[kb:]
     for d in range(2, nr, 2):
         got = send(after(pair, *a[2::2]), moved(d, 0))
         b[d], b[d + 1] = got[:kb], got[kb:]
@@ -130,18 +142,24 @@
     for d in range(nz):
         m[2 * d + 1] = my[d * kb : (d + 1) * kb]
     acx = jnp.where(row == z, half_of(a[0::2] + a[1::2], y), jnp.concatenate([px, pxy], axis=0))
-    ack = send(acx, moved(1, 0, core))
+    ack = send(acx, moved(1, 0))
 
-    smem = pl.BlockSpec(memory_space=pltpu.SMEM)
+    hbm = pl.BlockSpec(memory_space=pl.ANY)
     vmem = pl.BlockSpec(memory_space=pltpu.VMEM)
     limit = pltpu.CompilerParams(vmem_limit_bytes=40 * 1024 * 1024)
     tile = jax.ShapeDtypeStruct((tall, narrow), jnp.float32)
     part, mask = pl.pallas_call(
         functools.partial(direct, sizes),
         out_shape=(tile, tile),
-        in_specs=[smem, smem] + [vmem] * (nc + nr),
+        in_specs=[hbm, hbm] + [vmem] * (nc + nr),
         out_specs=(vmem, vmem),
-        scratch_shapes=[pltpu.VMEM((ka * nc, tall), jnp.float32), pltpu.VMEM((kb * nr, narrow), jnp.float32)],
+        scratch_shapes=[
+            pltpu.VMEM((ka * nc, tall), jnp.float32),
+            pltpu.VMEM((kb * nr, narrow), jnp.float32),
+            pltpu.SMEM((IRREPS,), jnp.int32),
+            pltpu.SMEM((IRREPS,), jnp.int32),
+            pltpu.SemaphoreType.DMA((2,)),
+        ],
         compiler_params=limit,
     )(occ_counts, vir_counts, *a, *b)
     return pl.pallas_call(

time: 29.4 us -> 27.3 us (0.929)
  starting transfers between devices: 22.1 us -> 17.4 us
  waiting for transfers between devices: 1.88 us -> 4.79 us
  Pallas kernels: 3.09 us -> 2.56 us
    ppermute x12, starting transfers between devices: 22.1 us -> 17.4 us  [send(): return lax.ppermute(value, ('row', 'col'), pairs)]
    ppermute x12, waiting for transfers between devices: 1.88 us -> 4.79 us  [send(): return lax.ppermute(value, ('row', 'col'), pairs)]
    pallas_call x1, Pallas kernels: 1.79 us -> 1.25 us  [per_device(): pl.pallas_call(functools.partial(direct, sizes), out_shape=(tile, tile),...]
  transfers between devices with their start and end apart: 12 -> 12, of which waited for: 3 -> 6; matrix products, arithmetic and copies ran while one was open for 4% -> 4% of each run, Pallas kernels for 6% -> 5%
where the time goes in v4:
time: 27.3 us; the launch traced here: 26.8 us
  starting transfers between devices  17.4 us (64%)
  waiting for transfers between devices  4.79 us (18%)
  Pallas kernels  2.56 us (9%)
  local copies, waits for them, and re-layouts  1.73 us (6%)
    ppermute x12, starting transfers between devices, send(): return lax.ppermute(value, ('row', 'col'), pairs)  17.4 us
    ppermute x12, waiting for transfers between devices, send(): return lax.ppermute(value, ('row', 'col'), pairs)  4.79 us
    unnamed x16, local copies, waits for them, and re-layouts  1.63 us
    pallas_call x1, Pallas kernels, per_device(): pl.pallas_call(functools.partial(mirrored, sizes), out_shape=tile, in_spe...  1.31 us
    pallas_call x1, Pallas kernels, per_device(): pl.pallas_call(functools.partial(direct, sizes), out_shape=(tile, tile),...  1.25 us
  transfers between devices with their start and end apart: 12, of which 6 were waited for; matrix products, arithmetic and copies ran while one was open for 4% of the time, Pallas kernels for 5%

profile of v4, /device:TPU:0, one launch (start us, length us, event | category | flops | bytes accessed | tf_op | source)
XLA Modules:
  0.0 26.8 jit_solution(16711139854551325643)
XLA Ops:
  0.0 3.0 %collective-permute-start = (f32[32,512]{1,0:T(8,128)}, f32[32,512]{1,0:T(8,128)S(1)}, u32[]{:S(2)}, u32[]{:S(2)}) collective-permute-start(f32[32,512]{1,0:T(8,128)} %bitcast.6), channel_id=1, source_target_pairs={{0,2},{1,3},{2,0},{3,1},{4,6},{5,7},{6,4},{7,5},{8,10},{9,11},{10,... | collective-permute-start | bytes 196616 | tf_op jit(solution)/shard_map/ppermute | solution.py:98
  3.0 2.6 %collective-permute-start.1 = (f32[32,512]{1,0:T(8,128)}, f32[32,512]{1,0:T(8,128)S(1)}, u32[]{:S(2)}, u32[]{:S(2)}) collective-permute-start(f32[32,512]{1,0:T(8,128)} %bitcast.7), channel_id=1, source_target_pairs={{0,4},{1,5},{2,6},{3,7},{4,0},{5,1},{6,2},{7,3},{8,12},{9,13},{10,... | collective-permute-start | bytes 196616 | tf_op jit(solution)/shard_map/ppermute | solution.py:98
  5.6 0.0 collective-permute-start.2
  5.6 0.0 collective-permute-start.4
  5.6 0.0 copy-start
  5.6 0.9 %constant_dynamic-update-slice_fusion.1 = f32[128,256]{1,0:T(8,128)S(1)} fusion(f32[64,256]{1,0:T(8,128)} %refs_10_.1), kind=kLoop, calls=%fused_computation.12 | loop fusion | bytes 131072
  6.5 0.0 copy-done
  6.6 0.5 %collective-permute-done.4.refs_11_ = f32[64,256]{1,0:T(8,128)S(1)} collective-permute-done((f32[64,256]{1,0:T(8,128)}, f32[64,256]{1,0:T(8,128)S(1)}, u32[]{:S(2)}, u32[]{:S(2)}) %collective-permute-start.4) | collective-permute-done | bytes 65568 | tf_op jit(solution)/shard_map/ppermute | solution.py:98
  7.1 0.9 %collective-permute-start.6 = (f32[128,256]{1,0:T(8,128)S(1)}, f32[128,256]{1,0:T(8,128)S(1)}, u32[]{:S(2)}, u32[]{:S(2)}) collective-permute-start(f32[128,256]{1,0:T(8,128)S(1)} %constant_dynamic-update-slice_fusion), channel_id=1, source_target_pairs={{0,2},{1,3},{2,10},{3,11},{4,18},{5,19},{6,26},{7,27},{8,0},{9,1},... | collective-permute-start | bytes 393224 | tf_op jit(solution)/shard_map/ppermute | solution.py:98
  8.0 2.4 %collective-permute-start.7 = (f32[128,256]{1,0:T(8,128)S(1)}, f32[128,256]{1,0:T(8,128)S(1)}, u32[]{:S(2)}, u32[]{:S(2)}) collective-permute-start(f32[128,256]{1,0:T(8,128)S(1)} %constant_dynamic-update-slice_fusion), channel_id=1, source_target_pairs={{0,4},{1,5},{2,12},{3,13},{4,20},{5,21},{6,28},{7,29},{8,6},{9,7},... | collective-permute-start | bytes 393224 | tf_op jit(solution)/shard_map/ppermute | solution.py:98
  10.4 0.0 collective-permute-done.refs_4_
  10.4 0.1 collective-permute-done.1.refs_6_
  10.5 1.5 %collective-permute-done.2.refs_8_ = f32[32,512]{1,0:T(8,128)S(1)} collective-permute-done((f32[32,512]{1,0:T(8,128)}, f32[32,512]{1,0:T(8,128)S(1)}, u32[]{:S(2)}, u32[]{:S(2)}) %collective-permute-start.2) | collective-permute-done | bytes 65568 | tf_op jit(solution)/shard_map/ppermute | solution.py:98
  12.0 1.6 %collective-permute-start.3 = (f32[128,512]{1,0:T(8,128)S(1)}, f32[128,512]{1,0:T(8,128)S(1)}, u32[]{:S(2)}, u32[]{:S(2)}) collective-permute-start(f32[128,512]{1,0:T(8,128)S(1)} %pad_maximum_fusion), channel_id=1, source_target_pairs={{0,1},{1,0},{2,3},{3,2},{4,5},{5,4},{6,7},{7,6},{8,9},{9,8},{10,11... | collective-permute-start | bytes 786440 | tf_op jit(solution)/shard_map/ppermute | solution.py:98
  13.7 3.3 %collective-permute-start.9 = (f32[128,256]{1,0:T(8,128)S(1)}, f32[128,256]{1,0:T(8,128)S(1)}, u32[]{:S(2)}, u32[]{:S(2)}) collective-permute-start(f32[128,256]{1,0:T(8,128)S(1)} %pad_maximum_fusion.2), channel_id=1, source_target_pairs={{0,16},{1,17},{10,26},{11,27},{20,4},{21,5},{30,14},{31,15}} | collective-permute-start | bytes 393224 | tf_op jit(solution)/shard_map/ppermute | solution.py:98
  17.0 1.3 %collective-permute-start.10 = (f32[128,256]{1,0:T(8,128)S(1)}, f32[128,256]{1,0:T(8,128)S(1)}, u32[]{:S(2)}, u32[]{:S(2)}) collective-permute-start(f32[128,256]{1,0:T(8,128)S(1)} %pad_maximum_fusion.3), channel_id=1, source_target_pairs={{0,17},{1,16},{10,27},{11,26},{20,5},{21,4},{30,15},{31,14}} | collective-permute-start | bytes 393224 | tf_op jit(solution)/shard_map/ppermute | solution.py:98
  18.3 0.0 collective-permute-done.6
  18.3 0.7 %collective-permute-start.5 = (f32[128,256]{1,0:T(8,128)S(1)}, f32[128,256]{1,0:T(8,128)S(1)}, u32[]{:S(2)}, u32[]{:S(2)}) collective-permute-start(f32[128,256]{1,0:T(8,128)S(1)} %constant_dynamic-update-slice_fusion), channel_id=1, source_target_pairs={{0,16},{1,17},{2,18},{3,19},{4,20},{5,21},{6,22},{7,23},{8,24},{9,... | collective-permute-start | bytes 393224 | tf_op jit(solution)/shard_map/ppermute | solution.py:98
  19.0 0.0 collective-permute-done.7
  19.1 1.6 %collective-permute-start.8 = (f32[256,256]{1,0:T(8,128)S(1)}, f32[256,256]{1,0:T(8,128)S(1)}, u32[]{:S(2)}, u32[]{:S(2)}) collective-permute-start(f32[256,256]{1,0:T(8,128)S(1)} %pad_maximum_fusion.1), channel_id=1, source_target_pairs={{0,1},{1,0},{2,3},{3,2},{4,5},{5,4},{6,7},{7,6},{8,9},{9,8},{10,11... | collective-permute-start | bytes 786440 | tf_op jit(solution)/shard_map/ppermute | solution.py:98
  20.6 0.0 collective-permute-done.3
  20.8 0.0 collective-permute-done.9
  20.8 0.5 %collective-permute-done.10 = f32[128,256]{1,0:T(8,128)S(1)} collective-permute-done((f32[128,256]{1,0:T(8,128)S(1)}, f32[128,256]{1,0:T(8,128)S(1)}, u32[]{:S(2)}, u32[]{:S(2)}) %collective-permute-start.10) | collective-permute-done | bytes 131104 | tf_op jit(solution)/shard_map/ppermute | solution.py:98
  21.3 0.0 copy-start.1
  21.3 0.1 collective-permute-start.11
  21.4 2.0 %collective-permute-done.5 = f32[128,256]{1,0:T(8,128)S(1)} collective-permute-done((f32[128,256]{1,0:T(8,128)S(1)}, f32[128,256]{1,0:T(8,128)S(1)}, u32[]{:S(2)}, u32[]{:S(2)}) %collective-permute-start.5) | collective-permute-done | bytes 131104 | tf_op jit(solution)/shard_map/ppermute | solution.py:98
  23.4 0.0 copy-start.2
  23.4 0.0 copy-start.3
  23.4 0.0 copy-done.1
  23.4 0.6 %copy-done.2 = s32[8]{0:T(128)S(1)} copy-done((s32[8]{0:T(128)S(1)}, s32[8]{0:T(128)}, u32[]{:S(2)}) %copy-start.2) | copy-done | bytes 56
  24.0 0.0 copy-done.3
  24.1 1.3 %shard_map.46 = (f32[512,256]{1,0:T(8,128)S(1)}, f32[512,256]{1,0:T(8,128)S(1)}) custom-call(s32[8]{0:T(128)S(1)} %copy-done.2, s32[8]{0:T(128)S(1)} %copy-done.3, f32[32,512]{1,0:T(8,128)S(1)} %bitcast.10, f32[32,512]{1,0:T(8,128)S(1)} %get-tuple-element.26.refs_3_, f32[32,512]{1,0:T(8,128)S(1)} %collective-permute-done.refs_4_, ...), custom_call_target="tpu_custom_call" | custom-call | tf_op jit(solution)/shard_map/pallas_call | solution.py:151
  25.3 0.2 collective-permute-done.8
  25.5 0.0 collective-permute-done.11.refs_11_
  25.5 1.3 %shard_map.47 = f32[512,256]{1,0:T(8,128)} custom-call(f32[512,256]{1,0:T(8,128)S(1)} %get-tuple-element.9.refs_0_, f32[512,256]{1,0:T(8,128)S(1)} %get-tuple-element.10.refs_1_, f32[64,256]{1,0:T(8,128)S(1)} %get-tuple-element.30.refs_2_, f32[64,256]{1,0:T(8,128)S(1)} %get-tuple-element.22.refs_3_, f32[64,256]{1,0:T(8,128)S(1)} %get-tuple-element.29.refs_4_, ...), custom_call_target="tpu_custom_call" | custom-call | tf_op jit(solution)/shard_map/pallas_call | solution.py:165
  (20 shorter events, 0.3 us)
Async XLA Ops:
  0.0 10.4 %collective-permute-start = (f32[32,512]{1,0:T(8,128)}, f32[32,512]{1,0:T(8,128)S(1)}, u32[]{:S(2)}, u32[]{:S(2)}) collective-permute-start(f32[32,512]{1,0:T(8,128)} %bitcast.6), channel_id=1, source_target_pairs={{0,2},{1,3},{2,0},{3,1},{4,6},{5,7},{6,4},{7,5},{8,10},{9,11},{10,... | collective-permute-start | bytes 196616 | tf_op jit(solution)/shard_map/ppermute | solution.py:98
  3.0 7.5 %collective-permute-start.1 = (f32[32,512]{1,0:T(8,128)}, f32[32,512]{1,0:T(8,128)S(1)}, u32[]{:S(2)}, u32[]{:S(2)}) collective-permute-start(f32[32,512]{1,0:T(8,128)} %bitcast.7), channel_id=1, source_target_pairs={{0,4},{1,5},{2,6},{3,7},{4,0},{5,1},{6,2},{7,3},{8,12},{9,13},{10,... | collective-permute-start | bytes 196616 | tf_op jit(solution)/shard_map/ppermute | solution.py:98
  5.6 6.4 %collective-permute-start.2 = (f32[32,512]{1,0:T(8,128)}, f32[32,512]{1,0:T(8,128)S(1)}, u32[]{:S(2)}, u32[]{:S(2)}) collective-permute-start(f32[32,512]{1,0:T(8,128)} %bitcast.8), channel_id=1, source_target_pairs={{0,6},{1,7},{2,4},{3,5},{4,2},{5,3},{6,0},{7,1},{8,14},{9,15},{10,... | collective-permute-start | bytes 196616 | tf_op jit(solution)/shard_map/ppermute | solution.py:98
  5.6 1.5 %collective-permute-start.4 = (f32[64,256]{1,0:T(8,128)}, f32[64,256]{1,0:T(8,128)S(1)}, u32[]{:S(2)}, u32[]{:S(2)}) collective-permute-start(f32[64,256]{1,0:T(8,128)} %refs_10_.1), channel_id=1, source_target_pairs={{0,8},{1,9},{2,10},{3,11},{4,12},{5,13},{6,14},{7,15},{8,0},{9,1},... | collective-permute-start | bytes 196616 | tf_op jit(solution)/shard_map/ppermute | solution.py:98
  5.6 0.9 %copy-start = (f32[512,32]{0,1:T(8,128)S(1)}, f32[512,32]{0,1:T(8,128)}, u32[]{:S(2)}) copy-start(f32[512,32]{0,1:T(8,128)} %param.4) | copy-start | bytes 196612
  7.1 11.2 %collective-permute-start.6 = (f32[128,256]{1,0:T(8,128)S(1)}, f32[128,256]{1,0:T(8,128)S(1)}, u32[]{:S(2)}, u32[]{:S(2)}) collective-permute-start(f32[128,256]{1,0:T(8,128)S(1)} %constant_dynamic-update-slice_fusion), channel_id=1, source_target_pairs={{0,2},{1,3},{2,10},{3,11},{4,18},{5,19},{6,26},{7,27},{8,0},{9,1},... | collective-permute-start | bytes 393224 | tf_op jit(solution)/shard_map/ppermute | solution.py:98
  8.0 11.0 %collective-permute-start.7 = (f32[128,256]{1,0:T(8,128)S(1)}, f32[128,256]{1,0:T(8,128)S(1)}, u32[]{:S(2)}, u32[]{:S(2)}) collective-permute-start(f32[128,256]{1,0:T(8,128)S(1)} %constant_dynamic-update-slice_fusion), channel_id=1, source_target_pairs={{0,4},{1,5},{2,12},{3,13},{4,20},{5,21},{6,28},{7,29},{8,6},{9,7},... | collective-permute-start | bytes 393224 | tf_op jit(solution)/shard_map/ppermute | solution.py:98
  12.0 8.6 %collective-permute-start.3 = (f32[128,512]{1,0:T(8,128)S(1)}, f32[128,512]{1,0:T(8,128)S(1)}, u32[]{:S(2)}, u32[]{:S(2)}) collective-permute-start(f32[128,512]{1,0:T(8,128)S(1)} %pad_maximum_fusion), channel_id=1, source_target_pairs={{0,1},{1,0},{2,3},{3,2},{4,5},{5,4},{6,7},{7,6},{8,9},{9,8},{10,11... | collective-permute-start | bytes 786440 | tf_op jit(solution)/shard_map/ppermute | solution.py:98
  13.7 7.1 %collective-permute-start.9 = (f32[128,256]{1,0:T(8,128)S(1)}, f32[128,256]{1,0:T(8,128)S(1)}, u32[]{:S(2)}, u32[]{:S(2)}) collective-permute-start(f32[128,256]{1,0:T(8,128)S(1)} %pad_maximum_fusion.2), channel_id=1, source_target_pairs={{0,16},{1,17},{10,26},{11,27},{20,4},{21,5},{30,14},{31,15}} | collective-permute-start | bytes 393224 | tf_op jit(solution)/shard_map/ppermute | solution.py:98
  17.0 4.3 %collective-permute-start.10 = (f32[128,256]{1,0:T(8,128)S(1)}, f32[128,256]{1,0:T(8,128)S(1)}, u32[]{:S(2)}, u32[]{:S(2)}) collective-permute-start(f32[128,256]{1,0:T(8,128)S(1)} %pad_maximum_fusion.3), channel_id=1, source_target_pairs={{0,17},{1,16},{10,27},{11,26},{20,5},{21,4},{30,15},{31,14}} | collective-permute-start | bytes 393224 | tf_op jit(solution)/shard_map/ppermute | solution.py:98
  18.3 5.0 %collective-permute-start.5 = (f32[128,256]{1,0:T(8,128)S(1)}, f32[128,256]{1,0:T(8,128)S(1)}, u32[]{:S(2)}, u32[]{:S(2)}) collective-permute-start(f32[128,256]{1,0:T(8,128)S(1)} %constant_dynamic-update-slice_fusion), channel_id=1, source_target_pairs={{0,16},{1,17},{2,18},{3,19},{4,20},{5,21},{6,22},{7,23},{8,24},{9,... | collective-permute-start | bytes 393224 | tf_op jit(solution)/shard_map/ppermute | solution.py:98
  19.1 6.4 %collective-permute-start.8 = (f32[256,256]{1,0:T(8,128)S(1)}, f32[256,256]{1,0:T(8,128)S(1)}, u32[]{:S(2)}, u32[]{:S(2)}) collective-permute-start(f32[256,256]{1,0:T(8,128)S(1)} %pad_maximum_fusion.1), channel_id=1, source_target_pairs={{0,1},{1,0},{2,3},{3,2},{4,5},{5,4},{6,7},{7,6},{8,9},{9,8},{10,11... | collective-permute-start | bytes 786440 | tf_op jit(solution)/shard_map/ppermute | solution.py:98
  21.3 2.1 %copy-start.1 = (f32[64,256]{1,0:T(8,128)S(1)}, f32[64,256]{1,0:T(8,128)}, u32[]{:S(2)}) copy-start(f32[64,256]{1,0:T(8,128)} %refs_10_.1) | copy-start | bytes 196612
  21.3 4.2 %collective-permute-start.11 = (f32[256,256]{1,0:T(8,128)S(1)}, f32[256,256]{1,0:T(8,128)S(1)}, u32[]{:S(2)}, u32[]{:S(2)}) collective-permute-start(f32[256,256]{1,0:T(8,128)S(1)} %maximum_select_fusion.refs_10_), channel_id=1, source_target_pairs={{0,8},{1,9},{2,10},{3,11},{4,12},{5,13},{6,14},{7,15},{8,0},{9,1},... | collective-permute-start | bytes 786440 | tf_op jit(solution)/shard_map/ppermute | solution.py:98
  23.4 0.7 %copy-start.2 = (s32[8]{0:T(128)S(1)}, s32[8]{0:T(128)}, u32[]{:S(2)}) copy-start(s32[8]{0:T(128)} %refs_0_.1) | copy-start | bytes 100
  23.4 0.7 %copy-start.3 = (s32[8]{0:T(128)S(1)}, s32[8]{0:T(128)}, u32[]{:S(2)}) copy-start(s32[8]{0:T(128)} %refs_1_.1) | copy-start | bytes 100

commit v5 on v4

v5 whole, which is shorter than its diff:
```python
import functools
import jax
import jax.numpy as jnp
from jax import lax
from jax.experimental import pallas as pl
from jax.experimental.pallas import tpu as pltpu
from jax.sharding import PartitionSpec as P

NVIR = 400
IRREPS = 8


def labels_of(pos, occ, vir):
    occ_of = pos // NVIR
    vir_of = pos - occ_of * NVIR
    one = jnp.zeros_like(pos)
    two = jnp.zeros_like(pos)
    for bound in occ:
        one = one + jnp.where(occ_of >= bound, 1, 0)
    for bound in vir:
        two = two + jnp.where(vir_of >= bound, 1, 0)
    return one ^ two


def halves(value):
    high = value.astype(jnp.bfloat16)
    return high, (value - high.astype(jnp.float32)).astype(jnp.bfloat16)


def product(left, right):
    def mm(one, two):
        return lax.dot_general(one, two, (((0,), (0,)), ((), ())), preferred_element_type=jnp.float32)

    (lh, ll), (rh, rl) = halves(left), halves(right)
    return mm(lh, rl) + mm(ll, rh) + mm(lh, rh)


def shifts_of(nz):
    return [e ^ 1 ^ (e // 2 % 2) for e in range(0, nz, 2)]


def direct(sizes, occ_hbm, vir_hbm, a_ref, ay_ref, *refs):
    nr, nc, tall, narrow, ka, kb = sizes
    b_refs = refs[: nr // 2]
    out_ref, mask_ref, left, right, occ_ref, vir_ref, sems = refs[nr // 2 :]
    copies = [
        pltpu.make_async_copy(occ_hbm, occ_ref, sems.at[0]),
        pltpu.make_async_copy(vir_hbm, vir_ref, sems.at[1]),
    ]
    for copy in copies:
        copy.start()
    row, col = lax.axis_index("row"), lax.axis_index("col")
    for d in range(nc // 2):
        rows = pl.ds(d * ka, ka)
        left[pl.ds(pl.multiple_of((col ^ (2 * d)) * ka, ka), ka), :] = a_ref[rows, :]
        left[pl.ds(pl.multiple_of((col ^ (2 * d + 1)) * ka, ka), ka), :] = ay_ref[rows, :]
    for d in range(nr):
        at = pl.multiple_of((row ^ d) * kb, kb)
        right[pl.ds(at, kb), :] = b_refs[d // 2][d % 2 * kb : (d % 2 + 1) * kb, :]
    out_ref[...] = product(left[...], right[...])
    for copy in copies:
        copy.wait()
    occ, vir = [], []
    one = two = 0
    for h in range(IRREPS - 1):
        one, two = one + occ_ref[h], two + vir_ref[h]
        occ.append(one)
        vir.append(two)
    rows = labels_of(row * tall + lax.broadcasted_iota(jnp.int32, (tall, 1), 0), occ, vir)
    cols = labels_of(col * narrow + lax.broadcasted_iota(jnp.int32, (1, narrow), 1), occ, vir)
    mask_ref[...] = jnp.where(rows == cols, 1.0, 0.0)


def mirrored(sizes, part_ref, mask_ref, my_ref, acx_ref, ack_ref, *refs):
    nr, nc, tall, narrow, ka, kb = sizes
    nz = nc // 2
    m_refs = refs[: nz // 2]
    out_ref, left, right = refs[nz // 2 :]
    row, col = lax.axis_index("row"), lax.axis_index("col")
    z, y = col // 2, lax.rem(col, 2)
    mine = lax.rem(row, 2) == lax.rem(z, 2)
    own_lane = pl.ds(pl.multiple_of(y * narrow, narrow), narrow)
    other_lane = pl.ds(pl.multiple_of((1 - y) * narrow, narrow), narrow)
    for i, e in enumerate(shifts_of(nz)):
        for j in range(2):
            at = pl.ds(pl.multiple_of((z ^ e ^ j) * kb, kb), kb)
            left[at, own_lane] = m_refs[i][j * kb : (j + 1) * kb, :]
            left[at, other_lane] = my_ref[(2 * i + j) * kb : (2 * i + j + 1) * kb, :]
    for d in range(nc):
        at = pl.multiple_of((col ^ d) * ka, ka)
        rows = pl.ds((d % 2 * nz + d // 2) * ka, ka)
        right[pl.ds(at, ka), :] = jnp.where(mine, acx_ref[rows, :], ack_ref[rows, :])
    total = part_ref[...] + product(left[...], right[...])
    out_ref[...] = jnp.where(mask_ref[...] > 0.0, total, 0.0)


def per_device(sizes, amplitudes, integrals, occ_counts, vir_counts):
    nr, nc, tall, narrow, ka, kb = sizes
    nz = nc // 2
    row, col = lax.axis_index("row"), lax.axis_index("col")
    z, y = col // 2, lax.rem(col, 2)

    def send(value, pairs):
        return lax.ppermute(value, ("row", "col"), pairs)

    def moved(dr, dc, keep=lambda r, c: True):
        return [(r * nc + c, (r ^ dr) * nc + (c ^ dc)) for r in range(nr) for c in range(nc) if keep(r, c)]

    def mirror(e):
        return [(r * nc + c, (c // 2) * nc + 2 * (r ^ e) + c % 2) for r in range(nr) for c in range(nc)]

    def after(value, *others):
        return lax.optimization_barrier((value, *others))[0]

    def half_of(chunks, part):
        return jnp.concatenate([lax.dynamic_slice_in_dim(v, part * narrow, narrow, 1) for v in chunks], axis=0)

    def home(r, c):
        return r == c // 2

    swapped = send(integrals, moved(1, 0))
    pair = jnp.concatenate([integrals, swapped], axis=0)
    at = amplitudes.T
    az = [send(at, moved(0, 2 * d)) for d in range(nz - 1, 0, -1)]
    a = [at] + az[::-1]
    acat = jnp.concatenate(a, axis=0)
    m = [send(after(pair, swapped), mirror(e)) for e in shifts_of(nz)]
    b, px = [pair], 0.0
    both = after(jnp.concatenate([pair, half_of(a, y)], axis=0), swapped)
    for d in range(2, nr, 2):
        got = send(both, moved(d, 0))
        b.append(got[: 2 * kb])
        px = px + jnp.where((row ^ d) == z, got[2 * kb :], 0.0)
    ay = send(acat, moved(0, 1))
    pxy = half_of(a, 1 - y)
    pxy = sum(send(pxy, moved(d, 1, home)) for d in range(2, nr, 2))
    my = send(after(jnp.concatenate(m, axis=0), *m), moved(0, 1))
    own = half_of(a + [ay[d * ka : (d + 1) * ka] for d in range(nz)], y)
    acx = jnp.where(row == z, own, jnp.concatenate([px, pxy], axis=0))
    ack = send(after(acx, pxy), moved(1, 0))

    hbm = pl.BlockSpec(memory_space=pltpu.HBM)
    vmem = pl.BlockSpec(memory_space=pltpu.VMEM)
    limit = pltpu.CompilerParams(vmem_limit_bytes=40 * 1024 * 1024)
    tile = jax.ShapeDtypeStruct((tall, narrow), jnp.float32)
    part, mask = pl.pallas_call(
        functools.partial(direct, sizes),
        out_shape=(tile, tile),
        in_specs=[hbm, hbm] + [vmem] * (2 + nr // 2),
        out_specs=(vmem, vmem),
        scratch_shapes=[
            pltpu.VMEM((ka * nc, tall), jnp.float32),
            pltpu.VMEM((kb * nr, narrow), jnp.float32),
            pltpu.SMEM((IRREPS,), jnp.int32),
            pltpu.SMEM((IRREPS,), jnp.int32),
            pltpu.SemaphoreType.DMA((2,)),
        ],
        compiler_params=limit,
    )(after(occ_counts, *b[1:], *m), vir_counts, acat, ay, *b)
    return pl.pallas_call(
        functools.partial(mirrored, sizes),
        out_shape=tile,
        in_specs=[vmem] * (5 + nz // 2),
        out_specs=vmem,
        scratch_shapes=[pltpu.VMEM((kb * nr, tall), jnp.float32), pltpu.VMEM((ka * nc, narrow), jnp.float32)],
        compiler_params=limit,
    )(part, mask, my, acx, ack, *m)


def solution(mesh):
    nr, nc = mesh.shape["row"], mesh.shape["col"]

    def whole(amplitudes, integrals, occ_counts, vir_counts):
        pairs, kw = amplitudes.shape
        sizes = (nr, nc, pairs // nr, pairs // nc, kw // nc, kw // nr)
        placed = (P("row", "col"), P("row", "col"), P(), P())
        return jax.shard_map(
            functools.partial(per_device, sizes), mesh=mesh, in_specs=placed, out_specs=P("row", "col"), check_vma=False
        )(amplitudes, integrals, occ_counts, vir_counts)

    return whole
```

time: 27.3 us -> 27.2 us (level); the launches traced: 26.8 us -> 27 us
  waiting for transfers between devices: 4.79 us -> 5.15 us
    ppermute x12 -> x11, waiting for transfers between devices: 4.79 us -> 5.15 us  [send(): return lax.ppermute(value, ('row', 'col'), pairs)]
    unnamed x16 -> x11, local copies, waits for them, and re-layouts: 1.63 us -> 1.5 us
    ppermute x12 -> x11, starting transfers between devices: 17.4 us -> 17.4 us  [send(): return lax.ppermute(value, ('row', 'col'), pairs)]
  transfers between devices with their start and end apart: 12 -> 11, of which waited for: 6 -> 5; matrix products, arithmetic and copies ran while one was open for 4% -> 4% of each run, Pallas kernels for 5% -> 5%
where the time goes in v5:
time: 27.2 us; the launch traced here: 27 us
  starting transfers between devices  17.4 us (64%)
  waiting for transfers between devices  5.15 us (19%)
  Pallas kernels  2.56 us (9%)
  local copies, waits for them, and re-layouts  1.6 us (6%)
    ppermute x11, starting transfers between devices, send(): return lax.ppermute(value, ('row', 'col'), pairs)  17.4 us
    ppermute x11, waiting for transfers between devices, send(): return lax.ppermute(value, ('row', 'col'), pairs)  5.15 us
    unnamed x11, local copies, waits for them, and re-layouts  1.5 us
    pallas_call x1, Pallas kernels, per_device(): pl.pallas_call(functools.partial(mirrored, sizes), out_shape=tile, in_spe...  1.3 us
    pallas_call x1, Pallas kernels, per_device(): pl.pallas_call(functools.partial(direct, sizes), out_shape=(tile, tile),...  1.26 us
  transfers between devices with their start and end apart: 11, of which 5 were waited for; matrix products, arithmetic and copies ran while one was open for 4% of the time, Pallas kernels for 5%

profile of v5, /device:TPU:0, one launch (start us, length us, event | category | flops | bytes accessed | tf_op | source)
XLA Modules:
  0.0 27.0 jit_solution(12094365645508056417)
XLA Ops:
  0.0 5.0 %collective-permute-start.3 = (f32[32,512]{1,0:T(8,128)}, f32[32,512]{1,0:T(8,128)S(1)}, u32[]{:S(2)}, u32[]{:S(2)}) collective-permute-start(f32[32,512]{1,0:T(8,128)} %bitcast.6), channel_id=1, source_target_pairs={{0,6},{1,7},{2,4},{3,5},{4,2},{5,3},{6,0},{7,1},{8,14},{9,15},{10,... | collective-permute-start | bytes 196616 | tf_op jit(solution)/shard_map/ppermute | solution.py:104
  5.0 0.0 collective-permute-start.2
  5.1 0.6 %collective-permute-start.1 = (f32[32,512]{1,0:T(8,128)}, f32[32,512]{1,0:T(8,128)S(1)}, u32[]{:S(2)}, u32[]{:S(2)}) collective-permute-start(f32[32,512]{1,0:T(8,128)} %bitcast.8), channel_id=1, source_target_pairs={{0,2},{1,3},{2,0},{3,1},{4,6},{5,7},{6,4},{7,5},{8,10},{9,11},{10,... | collective-permute-start | bytes 196616 | tf_op jit(solution)/shard_map/ppermute | solution.py:104
  5.6 0.0 collective-permute-start
  5.6 0.0 copy-start.2
  5.6 0.9 %constant_dynamic-update-slice_fusion.7 = (f32[128,256]{1,0:T(8,128)S(1)}, f32[256,256]{1,0:T(8,128)S(1)}) fusion(f32[64,256]{1,0:T(8,128)} %param.5), kind=kLoop, calls=%fused_computation.12 | loop fusion | bytes 196608
  6.5 0.0 copy-done.2
  6.6 0.5 %collective-permute-done = f32[64,256]{1,0:T(8,128)S(1)} collective-permute-done((f32[64,256]{1,0:T(8,128)}, f32[64,256]{1,0:T(8,128)S(1)}, u32[]{:S(2)}, u32[]{:S(2)}) %collective-permute-start) | collective-permute-done | bytes 65568 | tf_op jit(solution)/shard_map/ppermute | solution.py:104
  7.1 1.5 %collective-permute-start.5 = (f32[128,256]{1,0:T(8,128)S(1)}, f32[128,256]{1,0:T(8,128)S(1)}, u32[]{:S(2)}, u32[]{:S(2)}) collective-permute-start(f32[128,256]{1,0:T(8,128)S(1)} %get-tuple-element.13.refs_0_), channel_id=1, source_target_pairs={{0,2},{1,3},{2,10},{3,11},{4,18},{5,19},{6,26},{7,27},{8,0},{9,1},... | collective-permute-start | bytes 393224 | tf_op jit(solution)/shard_map/ppermute | solution.py:104
  8.6 2.4 %collective-permute-start.6 = (f32[128,256]{1,0:T(8,128)S(1)}, f32[128,256]{1,0:T(8,128)S(1)}, u32[]{:S(2)}, u32[]{:S(2)}) collective-permute-start(f32[128,256]{1,0:T(8,128)S(1)} %get-tuple-element.13.refs_0_), channel_id=1, source_target_pairs={{0,4},{1,5},{2,12},{3,13},{4,20},{5,21},{6,28},{7,29},{8,6},{9,7},... | collective-permute-start | bytes 393224 | tf_op jit(solution)/shard_map/ppermute | solution.py:104
  11.0 0.0 collective-permute-done.3
  11.0 0.0 collective-permute-done.2
  11.0 0.0 collective-permute-done.1
  11.1 1.6 %collective-permute-start.7 = (f32[128,512]{1,0:T(8,128)S(1)}, f32[128,512]{1,0:T(8,128)S(1)}, u32[]{:S(2)}, u32[]{:S(2)}) collective-permute-start(f32[128,512]{1,0:T(8,128)S(1)} %pad_maximum_fusion.a_ref), channel_id=1, source_target_pairs={{0,1},{1,0},{2,3},{3,2},{4,5},{5,4},{6,7},{7,6},{8,9},{9,8},{10,11... | collective-permute-start | bytes 786440 | tf_op jit(solution)/shard_map/ppermute | solution.py:104
  12.7 1.5 %collective-permute-start.4 = (f32[256,256]{1,0:T(8,128)S(1)}, f32[256,256]{1,0:T(8,128)S(1)}, u32[]{:S(2)}, u32[]{:S(2)}) collective-permute-start(f32[256,256]{1,0:T(8,128)S(1)} %get-tuple-element.12), channel_id=1, source_target_pairs={{0,16},{1,17},{2,18},{3,19},{4,20},{5,21},{6,22},{7,23},{8,24},{9,... | collective-permute-start | bytes 786440 | tf_op jit(solution)/shard_map/ppermute | solution.py:104
  14.2 2.4 %collective-permute-start.9 = (f32[128,256]{1,0:T(8,128)S(1)}, f32[128,256]{1,0:T(8,128)S(1)}, u32[]{:S(2)}, u32[]{:S(2)}) collective-permute-start(f32[128,256]{1,0:T(8,128)S(1)} %pad_maximum_fusion.2), channel_id=1, source_target_pairs={{0,17},{1,16},{10,27},{11,26},{20,5},{21,4},{30,15},{31,14}} | collective-permute-start | bytes 393224 | tf_op jit(solution)/shard_map/ppermute | solution.py:104
  16.7 0.0 collective-permute-done.5.refs_0_
  16.7 0.5 %collective-permute-done.6.refs_1_ = f32[128,256]{1,0:T(8,128)S(1)} collective-permute-done((f32[128,256]{1,0:T(8,128)S(1)}, f32[128,256]{1,0:T(8,128)S(1)}, u32[]{:S(2)}, u32[]{:S(2)}) %collective-permute-start.6) | collective-permute-done | bytes 131104 | tf_op jit(solution)/shard_map/ppermute | solution.py:104
  17.2 2.3 %collective-permute-start.8 = (f32[256,256]{1,0:T(8,128)S(1)}, f32[256,256]{1,0:T(8,128)S(1)}, u32[]{:S(2)}, u32[]{:S(2)}) collective-permute-start(f32[256,256]{1,0:T(8,128)S(1)} %pad_maximum_fusion.1), channel_id=1, source_target_pairs={{0,1},{1,0},{2,3},{3,2},{4,5},{5,4},{6,7},{7,6},{8,9},{9,8},{10,11... | collective-permute-start | bytes 786440 | tf_op jit(solution)/shard_map/ppermute | solution.py:104
  19.5 0.8 %collective-permute-done.7.ay_ref = f32[128,512]{1,0:T(8,128)S(1)} collective-permute-done((f32[128,512]{1,0:T(8,128)S(1)}, f32[128,512]{1,0:T(8,128)S(1)}, u32[]{:S(2)}, u32[]{:S(2)}) %collective-permute-start.7) | collective-permute-done | bytes 262176 | tf_op jit(solution)/shard_map/ppermute | solution.py:104
  20.4 1.8 %collective-permute-done.4 = f32[256,256]{1,0:T(8,128)S(1)} collective-permute-done((f32[256,256]{1,0:T(8,128)S(1)}, f32[256,256]{1,0:T(8,128)S(1)}, u32[]{:S(2)}, u32[]{:S(2)}) %collective-permute-start.4) | collective-permute-done | bytes 262176 | tf_op jit(solution)/shard_map/ppermute | solution.py:104
  22.2 0.0 collective-permute-done.9
  22.3 0.0 copy-start
  22.3 0.0 copy-start.1
  22.3 0.1 collective-permute-start.10
  22.4 0.6 %copy-done = s32[8]{0:T(128)S(1)} copy-done((s32[8]{0:T(128)S(1)}, s32[8]{0:T(128)}, u32[]{:S(2)}) %copy-start) | copy-done | bytes 56
  22.9 0.0 copy-done.1
  23.0 1.3 %shard_map.46 = (f32[512,256]{1,0:T(8,128)S(1)}, f32[512,256]{1,0:T(8,128)S(1)}) custom-call(s32[8]{0:T(128)S(1)} %copy-done, s32[8]{0:T(128)S(1)} %copy-done.1, f32[128,512]{1,0:T(8,128)S(1)} %pad_maximum_fusion.a_ref, f32[128,512]{1,0:T(8,128)S(1)} %collective-permute-done.7.ay_ref, f32[128,256]{1,0:T(8,128)S(1)} %get-tuple-element.13.refs_0_, ...), custom_call_target="tpu_custom_call" | custom-call | tf_op jit(solution)/shard_map/pallas_call | solution.py:146
  24.2 1.5 %collective-permute-done.8.my_ref = f32[256,256]{1,0:T(8,128)S(1)} collective-permute-done((f32[256,256]{1,0:T(8,128)S(1)}, f32[256,256]{1,0:T(8,128)S(1)}, u32[]{:S(2)}, u32[]{:S(2)}) %collective-permute-start.8) | collective-permute-done | bytes 262176 | tf_op jit(solution)/shard_map/ppermute | solution.py:104
  25.7 0.0 collective-permute-done.10.ack_ref
  25.7 1.3 %shard_map.47 = f32[512,256]{1,0:T(8,128)} custom-call(f32[512,256]{1,0:T(8,128)S(1)} %get-tuple-element.15.part_ref, f32[512,256]{1,0:T(8,128)S(1)} %get-tuple-element.16.mask_ref, f32[256,256]{1,0:T(8,128)S(1)} %collective-permute-done.8.my_ref, f32[256,256]{1,0:T(8,128)S(1)} %maximum_select_fusion.acx_ref, ...), custom_call_target="tpu_custom_call" | custom-call | tf_op jit(solution)/shard_map/pallas_call | solution.py:160
  (16 shorter events, 0.2 us)
Async XLA Ops:
  0.0 11.0 %collective-permute-start.3 = (f32[32,512]{1,0:T(8,128)}, f32[32,512]{1,0:T(8,128)S(1)}, u32[]{:S(2)}, u32[]{:S(2)}) collective-permute-start(f32[32,512]{1,0:T(8,128)} %bitcast.6), channel_id=1, source_target_pairs={{0,6},{1,7},{2,4},{3,5},{4,2},{5,3},{6,0},{7,1},{8,14},{9,15},{10,... | collective-permute-start | bytes 196616 | tf_op jit(solution)/shard_map/ppermute | solution.py:104
  5.0 6.0 %collective-permute-start.2 = (f32[32,512]{1,0:T(8,128)}, f32[32,512]{1,0:T(8,128)S(1)}, u32[]{:S(2)}, u32[]{:S(2)}) collective-permute-start(f32[32,512]{1,0:T(8,128)} %bitcast.7), channel_id=1, source_target_pairs={{0,4},{1,5},{2,6},{3,7},{4,0},{5,1},{6,2},{7,3},{8,12},{9,13},{10,... | collective-permute-start | bytes 196616 | tf_op jit(solution)/shard_map/ppermute | solution.py:104
  5.1 6.0 %collective-permute-start.1 = (f32[32,512]{1,0:T(8,128)}, f32[32,512]{1,0:T(8,128)S(1)}, u32[]{:S(2)}, u32[]{:S(2)}) collective-permute-start(f32[32,512]{1,0:T(8,128)} %bitcast.8), channel_id=1, source_target_pairs={{0,2},{1,3},{2,0},{3,1},{4,6},{5,7},{6,4},{7,5},{8,10},{9,11},{10,... | collective-permute-start | bytes 196616 | tf_op jit(solution)/shard_map/ppermute | solution.py:104
  5.6 1.5 %collective-permute-start = (f32[64,256]{1,0:T(8,128)}, f32[64,256]{1,0:T(8,128)S(1)}, u32[]{:S(2)}, u32[]{:S(2)}) collective-permute-start(f32[64,256]{1,0:T(8,128)} %param.5), channel_id=1, source_target_pairs={{0,8},{1,9},{2,10},{3,11},{4,12},{5,13},{6,14},{7,15},{8,0},{9,1},... | collective-permute-start | bytes 196616 | tf_op jit(solution)/shard_map/ppermute | solution.py:104
  5.6 0.9 %copy-start.2 = (f32[512,32]{0,1:T(8,128)S(1)}, f32[512,32]{0,1:T(8,128)}, u32[]{:S(2)}) copy-start(f32[512,32]{0,1:T(8,128)} %param.4) | copy-start | bytes 196612
  7.1 9.6 %collective-permute-start.5 = (f32[128,256]{1,0:T(8,128)S(1)}, f32[128,256]{1,0:T(8,128)S(1)}, u32[]{:S(2)}, u32[]{:S(2)}) collective-permute-start(f32[128,256]{1,0:T(8,128)S(1)} %get-tuple-element.13.refs_0_), channel_id=1, source_target_pairs={{0,2},{1,3},{2,10},{3,11},{4,18},{5,19},{6,26},{7,27},{8,0},{9,1},... | collective-permute-start | bytes 393224 | tf_op jit(solution)/shard_map/ppermute | solution.py:104
  8.6 8.6 %collective-permute-start.6 = (f32[128,256]{1,0:T(8,128)S(1)}, f32[128,256]{1,0:T(8,128)S(1)}, u32[]{:S(2)}, u32[]{:S(2)}) collective-permute-start(f32[128,256]{1,0:T(8,128)S(1)} %get-tuple-element.13.refs_0_), channel_id=1, source_target_pairs={{0,4},{1,5},{2,12},{3,13},{4,20},{5,21},{6,28},{7,29},{8,6},{9,7},... | collective-permute-start | bytes 393224 | tf_op jit(solution)/shard_map/ppermute | solution.py:104
  11.1 9.2 %collective-permute-start.7 = (f32[128,512]{1,0:T(8,128)S(1)}, f32[128,512]{1,0:T(8,128)S(1)}, u32[]{:S(2)}, u32[]{:S(2)}) collective-permute-start(f32[128,512]{1,0:T(8,128)S(1)} %pad_maximum_fusion.a_ref), channel_id=1, source_target_pairs={{0,1},{1,0},{2,3},{3,2},{4,5},{5,4},{6,7},{7,6},{8,9},{9,8},{10,11... | collective-permute-start | bytes 786440 | tf_op jit(solution)/shard_map/ppermute | solution.py:104
  12.7 9.5 %collective-permute-start.4 = (f32[256,256]{1,0:T(8,128)S(1)}, f32[256,256]{1,0:T(8,128)S(1)}, u32[]{:S(2)}, u32[]{:S(2)}) collective-permute-start(f32[256,256]{1,0:T(8,128)S(1)} %get-tuple-element.12), channel_id=1, source_target_pairs={{0,16},{1,17},{2,18},{3,19},{4,20},{5,21},{6,22},{7,23},{8,24},{9,... | collective-permute-start | bytes 786440 | tf_op jit(solution)/shard_map/ppermute | solution.py:104
  14.2 8.0 %collective-permute-start.9 = (f32[128,256]{1,0:T(8,128)S(1)}, f32[128,256]{1,0:T(8,128)S(1)}, u32[]{:S(2)}, u32[]{:S(2)}) collective-permute-start(f32[128,256]{1,0:T(8,128)S(1)} %pad_maximum_fusion.2), channel_id=1, source_target_pairs={{0,17},{1,16},{10,27},{11,26},{20,5},{21,4},{30,15},{31,14}} | collective-permute-start | bytes 393224 | tf_op jit(solution)/shard_map/ppermute | solution.py:104
  17.2 8.5 %collective-permute-start.8 = (f32[256,256]{1,0:T(8,128)S(1)}, f32[256,256]{1,0:T(8,128)S(1)}, u32[]{:S(2)}, u32[]{:S(2)}) collective-permute-start(f32[256,256]{1,0:T(8,128)S(1)} %pad_maximum_fusion.1), channel_id=1, source_target_pairs={{0,1},{1,0},{2,3},{3,2},{4,5},{5,4},{6,7},{7,6},{8,9},{9,8},{10,11... | collective-permute-start | bytes 786440 | tf_op jit(solution)/shard_map/ppermute | solution.py:104
  22.3 0.7 %copy-start = (s32[8]{0:T(128)S(1)}, s32[8]{0:T(128)}, u32[]{:S(2)}) copy-start(s32[8]{0:T(128)} %occ_hbm) | copy-start | bytes 100
  22.3 0.7 %copy-start.1 = (s32[8]{0:T(128)S(1)}, s32[8]{0:T(128)}, u32[]{:S(2)}) copy-start(s32[8]{0:T(128)} %vir_hbm.1) | copy-start | bytes 100
  22.3 3.4 %collective-permute-start.10 = (f32[256,256]{1,0:T(8,128)S(1)}, f32[256,256]{1,0:T(8,128)S(1)}, u32[]{:S(2)}, u32[]{:S(2)}) collective-permute-start(f32[256,256]{1,0:T(8,128)S(1)} %maximum_select_fusion.acx_ref), channel_id=1, source_target_pairs={{0,8},{1,9},{2,10},{3,11},{4,12},{5,13},{6,14},{7,15},{8,0},{9,1},... | collective-permute-start | bytes 786440 | tf_op jit(solution)/shard_map/ppermute | solution.py:104

commit v6 on v5

--- a/solution.py
+++ b/solution.py
@@ -31,7 +31,7 @@
     def mm(one, two):
         return lax.dot_general(one, two, (((0,), (0,)), ((), ())), preferred_element_type=jnp.float32)
 
-    (lh, ll), (rh, rl) = halves(left), halves(right)
+    (lh, ll), (rh, rl) = left, right
     return mm(lh, rl) + mm(ll, rh) + mm(lh, rh)
 
 
@@ -57,7 +57,7 @@
     for d in range(nr):
         at = pl.multiple_of((row ^ d) * kb, kb)
         right[pl.ds(at, kb), :] = b_refs[d // 2][d % 2 * kb : (d % 2 + 1) * kb, :]
-    out_ref[...] = product(left[...], right[...])
+    out_ref[...] = product(halves(left[...]), halves(right[...]))
     for copy in copies:
         copy.wait()
     occ, vir = [], []
@@ -75,23 +75,25 @@
     nr, nc, tall, narrow, ka, kb = sizes
     nz = nc // 2
     m_refs = refs[: nz // 2]
-    out_ref, left, right = refs[nz // 2 :]
+    out_hbm, right, done, sems = refs[nz // 2 :]
     row, col = lax.axis_index("row"), lax.axis_index("col")
     z, y = col // 2, lax.rem(col, 2)
     mine = lax.rem(row, 2) == lax.rem(z, 2)
-    own_lane = pl.ds(pl.multiple_of(y * narrow, narrow), narrow)
-    other_lane = pl.ds(pl.multiple_of((1 - y) * narrow, narrow), narrow)
-    for i, e in enumerate(shifts_of(nz)):
-        for j in range(2):
-            at = pl.ds(pl.multiple_of((z ^ e ^ j) * kb, kb), kb)
-            left[at, own_lane] = m_refs[i][j * kb : (j + 1) * kb, :]
-            left[at, other_lane] = my_ref[(2 * i + j) * kb : (2 * i + j + 1) * kb, :]
+    chunks = [e ^ j for e in shifts_of(nz) for j in range(2)]
     for d in range(nc):
-        at = pl.multiple_of((col ^ d) * ka, ka)
+        at = pl.multiple_of((2 * chunks.index(d // 2) + (y ^ (d % 2))) * ka, ka)
         rows = pl.ds((d % 2 * nz + d // 2) * ka, ka)
         right[pl.ds(at, ka), :] = jnp.where(mine, acx_ref[rows, :], ack_ref[rows, :])
-    total = part_ref[...] + product(left[...], right[...])
-    out_ref[...] = jnp.where(mask_ref[...] > 0.0, total, 0.0)
+    right_halves = halves(right[...])
+    stores = []
+    for half, left in enumerate((jnp.concatenate([m_ref[...] for m_ref in m_refs], axis=0), my_ref[...])):
+        rows = pl.ds(pl.multiple_of((y ^ half) * narrow, narrow), narrow)
+        total = part_ref[rows, :] + product(halves(left), right_halves)
+        done[half] = jnp.where(mask_ref[rows, :] > 0.0, total, 0.0)
+        stores.append(pltpu.make_async_copy(done.at[half], out_hbm.at[rows, :], sems.at[half]))
+        stores[half].start()
+    for store in stores:
+        store.wait()
 
 
 def per_device(sizes, amplitudes, integrals, occ_counts, vir_counts):
@@ -124,20 +126,20 @@
     az = [send(at, moved(0, 2 * d)) for d in range(nz - 1, 0, -1)]
     a = [at] + az[::-1]
     acat = jnp.concatenate(a, axis=0)
-    m = [send(after(pair, swapped), mirror(e)) for e in shifts_of(nz)]
+    m = [send(pair, mirror(e)) for e in shifts_of(nz)]
     b, px = [pair], 0.0
-    both = after(jnp.concatenate([pair, half_of(a, y)], axis=0), swapped)
+    both = jnp.concatenate([pair, half_of(a, y)], axis=0)
     for d in range(2, nr, 2):
         got = send(both, moved(d, 0))
         b.append(got[: 2 * kb])
         px = px + jnp.where((row ^ d) == z, got[2 * kb :], 0.0)
     ay = send(acat, moved(0, 1))
-    pxy = half_of(a, 1 - y)
+    pxy = after(half_of(a, 1 - y), swapped)
     pxy = sum(send(pxy, moved(d, 1, home)) for d in range(2, nr, 2))
-    my = send(after(jnp.concatenate(m, axis=0), *m), moved(0, 1))
+    my = send(after(jnp.concatenate(m, axis=0), *az), moved(0, 1))
     own = half_of(a + [ay[d * ka : (d + 1) * ka] for d in range(nz)], y)
     acx = jnp.where(row == z, own, jnp.concatenate([px, pxy], axis=0))
-    ack = send(after(acx, pxy), moved(1, 0))
+    ack = send(after(acx, *m), moved(1, 0))
 
     hbm = pl.BlockSpec(memory_space=pltpu.HBM)
     vmem = pl.BlockSpec(memory_space=pltpu.VMEM)
@@ -156,13 +158,17 @@
             pltpu.SemaphoreType.DMA((2,)),
         ],
         compiler_params=limit,
-    )(after(occ_counts, *b[1:], *m), vir_counts, acat, ay, *b)
+    )(occ_counts, vir_counts, acat, ay, *b)
     return pl.pallas_call(
         functools.partial(mirrored, sizes),
         out_shape=tile,
         in_specs=[vmem] * (5 + nz // 2),
-        out_specs=vmem,
-        scratch_shapes=[pltpu.VMEM((kb * nr, tall), jnp.float32), pltpu.VMEM((ka * nc, narrow), jnp.float32)],
+        out_specs=hbm,
+        scratch_shapes=[
+            pltpu.VMEM((ka * nc, narrow), jnp.float32),
+            pltpu.VMEM((2, narrow, narrow), jnp.float32),
+            pltpu.SemaphoreType.DMA((2,)),
+        ],
         compiler_params=limit,
     )(part, mask, my, acx, ack, *m)
 

time: 27.2 us -> 26.8 us (0.985)
  starting transfers between devices: 17.4 us -> 15.8 us
  waiting for transfers between devices: 5.15 us -> 6.41 us
    ppermute x11, starting transfers between devices: 17.4 us -> 15.8 us  [send(): return lax.ppermute(value, ('row', 'col'), pairs)]
    ppermute x11, waiting for transfers between devices: 5.15 us -> 6.41 us  [send(): return lax.ppermute(value, ('row', 'col'), pairs)]
    unnamed x11 -> x12, local copies, waits for them, and re-layouts: 1.5 us -> 1.51 us
  transfers between devices with their start and end apart: 11 -> 11, of which waited for: 5 -> 6; matrix products, arithmetic and copies ran while one was open for 4% -> 4% of each run, Pallas kernels for 5% -> 5%
where the time goes in v6:
time: 26.8 us; the launch traced here: 26.6 us
  starting transfers between devices  15.8 us (59%)
  waiting for transfers between devices  6.41 us (24%)
  Pallas kernels  2.48 us (9%)
  local copies, waits for them, and re-layouts  1.6 us (6%)
    ppermute x11, starting transfers between devices, send(): return lax.ppermute(value, ('row', 'col'), pairs)  15.8 us
    ppermute x11, waiting for transfers between devices, send(): return lax.ppermute(value, ('row', 'col'), pairs)  6.41 us
    unnamed x12, local copies, waits for them, and re-layouts  1.51 us
    pallas_call x1, Pallas kernels, per_device(): pl.pallas_call(functools.partial(direct, sizes), out_shape=(tile, tile),...  1.26 us
    pallas_call x1, Pallas kernels, per_device(): pl.pallas_call(functools.partial(mirrored, sizes), out_shape=tile, in_spe...  1.23 us
  transfers between devices with their start and end apart: 11, of which 6 were waited for; matrix products, arithmetic and copies ran while one was open for 4% of the time, Pallas kernels for 5%

profile of v6, /device:TPU:0, one launch (start us, length us, event | category | flops | bytes accessed | tf_op | source)
XLA Modules:
  0.0 26.6 jit_solution(6112773139291249130)
XLA Ops:
  0.0 5.0 %collective-permute-start.2 = (f32[32,512]{1,0:T(8,128)}, f32[32,512]{1,0:T(8,128)S(1)}, u32[]{:S(2)}, u32[]{:S(2)}) collective-permute-start(f32[32,512]{1,0:T(8,128)} %bitcast.6), channel_id=1, source_target_pairs={{0,6},{1,7},{2,4},{3,5},{4,2},{5,3},{6,0},{7,1},{8,14},{9,15},{10,... | collective-permute-start | bytes 196616 | tf_op jit(solution)/shard_map/ppermute | solution.py:106
  5.0 0.0 collective-permute-start.1
  5.1 0.6 %collective-permute-start = (f32[32,512]{1,0:T(8,128)}, f32[32,512]{1,0:T(8,128)S(1)}, u32[]{:S(2)}, u32[]{:S(2)}) collective-permute-start(f32[32,512]{1,0:T(8,128)} %bitcast.8), channel_id=1, source_target_pairs={{0,2},{1,3},{2,0},{3,1},{4,6},{5,7},{6,4},{7,5},{8,10},{9,11},{10,... | collective-permute-start | bytes 196616 | tf_op jit(solution)/shard_map/ppermute | solution.py:106
  5.6 0.0 collective-permute-start.4
  5.6 0.0 copy-start.2
  5.6 0.9 %constant_dynamic-update-slice_fusion.7 = (f32[256,256]{1,0:T(8,128)S(1)}, f32[128,256]{1,0:T(8,128)S(1)}) fusion(f32[64,256]{1,0:T(8,128)} %param.5), kind=kLoop, calls=%fused_computation.12 | loop fusion | bytes 196608
  6.5 0.0 copy-done.2
  6.6 0.5 %collective-permute-done.4 = f32[64,256]{1,0:T(8,128)S(1)} collective-permute-done((f32[64,256]{1,0:T(8,128)}, f32[64,256]{1,0:T(8,128)S(1)}, u32[]{:S(2)}, u32[]{:S(2)}) %collective-permute-start.4) | collective-permute-done | bytes 65568 | tf_op jit(solution)/shard_map/ppermute | solution.py:106
  7.1 2.4 %collective-permute-start.7 = (f32[128,256]{1,0:T(8,128)S(1)}, f32[128,256]{1,0:T(8,128)S(1)}, u32[]{:S(2)}, u32[]{:S(2)}) collective-permute-start(f32[128,256]{1,0:T(8,128)S(1)} %get-tuple-element.33.refs_0_), channel_id=1, source_target_pairs={{0,4},{1,5},{2,12},{3,13},{4,20},{5,21},{6,28},{7,29},{8,6},{9,7},... | collective-permute-start | bytes 393224 | tf_op jit(solution)/shard_map/ppermute | solution.py:106
  9.5 0.3 %collective-permute-start.6 = (f32[128,256]{1,0:T(8,128)S(1)}, f32[128,256]{1,0:T(8,128)S(1)}, u32[]{:S(2)}, u32[]{:S(2)}) collective-permute-start(f32[128,256]{1,0:T(8,128)S(1)} %get-tuple-element.33.refs_0_), channel_id=1, source_target_pairs={{0,2},{1,3},{2,10},{3,11},{4,18},{5,19},{6,26},{7,27},{8,0},{9,1},... | collective-permute-start | bytes 393224 | tf_op jit(solution)/shard_map/ppermute | solution.py:106
  9.8 0.0 collective-permute-done.2
  9.8 1.0 %collective-permute-done.1 = f32[32,512]{1,0:T(8,128)S(1)} collective-permute-done((f32[32,512]{1,0:T(8,128)}, f32[32,512]{1,0:T(8,128)S(1)}, u32[]{:S(2)}, u32[]{:S(2)}) %collective-permute-start.1) | collective-permute-done | bytes 65568 | tf_op jit(solution)/shard_map/ppermute | solution.py:106
  10.9 0.0 collective-permute-done
  10.9 1.6 %collective-permute-start.3 = (f32[128,512]{1,0:T(8,128)S(1)}, f32[128,512]{1,0:T(8,128)S(1)}, u32[]{:S(2)}, u32[]{:S(2)}) collective-permute-start(f32[128,512]{1,0:T(8,128)S(1)} %pad_maximum_fusion.a_ref), channel_id=1, source_target_pairs={{0,1},{1,0},{2,3},{3,2},{4,5},{5,4},{6,7},{7,6},{8,9},{9,8},{10,11... | collective-permute-start | bytes 786440 | tf_op jit(solution)/shard_map/ppermute | solution.py:106
  12.5 2.3 %collective-permute-start.5 = (f32[256,256]{1,0:T(8,128)S(1)}, f32[256,256]{1,0:T(8,128)S(1)}, u32[]{:S(2)}, u32[]{:S(2)}) collective-permute-start(f32[256,256]{1,0:T(8,128)S(1)} %get-tuple-element.29), channel_id=1, source_target_pairs={{0,16},{1,17},{2,18},{3,19},{4,20},{5,21},{6,22},{7,23},{8,24},{9,... | collective-permute-start | bytes 786440 | tf_op jit(solution)/shard_map/ppermute | solution.py:106
  14.9 1.9 %collective-permute-start.9 = (f32[128,256]{1,0:T(8,128)S(1)}, f32[128,256]{1,0:T(8,128)S(1)}, u32[]{:S(2)}, u32[]{:S(2)}) collective-permute-start(f32[128,256]{1,0:T(8,128)S(1)} %pad_maximum_fusion.2), channel_id=1, source_target_pairs={{0,17},{1,16},{10,27},{11,26},{20,5},{21,4},{30,15},{31,14}} | collective-permute-start | bytes 393224 | tf_op jit(solution)/shard_map/ppermute | solution.py:106
  16.8 0.0 collective-permute-done.7.refs_1_
  16.8 0.0 collective-permute-done.6.refs_0_
  16.8 1.6 %collective-permute-start.8 = (f32[256,256]{1,0:T(8,128)S(1)}, f32[256,256]{1,0:T(8,128)S(1)}, u32[]{:S(2)}, u32[]{:S(2)}) collective-permute-start(f32[256,256]{1,0:T(8,128)S(1)} %pad_maximum_fusion.1), channel_id=1, source_target_pairs={{0,1},{1,0},{2,3},{3,2},{4,5},{5,4},{6,7},{7,6},{8,9},{9,8},{10,11... | collective-permute-start | bytes 786440 | tf_op jit(solution)/shard_map/ppermute | solution.py:106
  18.4 1.0 %collective-permute-done.3.ay_ref = f32[128,512]{1,0:T(8,128)S(1)} collective-permute-done((f32[128,512]{1,0:T(8,128)S(1)}, f32[128,512]{1,0:T(8,128)S(1)}, u32[]{:S(2)}, u32[]{:S(2)}) %collective-permute-start.3) | collective-permute-done | bytes 262176 | tf_op jit(solution)/shard_map/ppermute | solution.py:106
  19.5 1.9 %collective-permute-done.5 = f32[256,256]{1,0:T(8,128)S(1)} collective-permute-done((f32[256,256]{1,0:T(8,128)S(1)}, f32[256,256]{1,0:T(8,128)S(1)}, u32[]{:S(2)}, u32[]{:S(2)}) %collective-permute-start.5) | collective-permute-done | bytes 262176 | tf_op jit(solution)/shard_map/ppermute | solution.py:106
  21.4 1.3 %collective-permute-done.9 = f32[128,256]{1,0:T(8,128)S(1)} collective-permute-done((f32[128,256]{1,0:T(8,128)S(1)}, f32[128,256]{1,0:T(8,128)S(1)}, u32[]{:S(2)}, u32[]{:S(2)}) %collective-permute-start.9) | collective-permute-done | bytes 131104 | tf_op jit(solution)/shard_map/ppermute | solution.py:106
  22.8 0.0 copy-start
  22.8 0.0 copy-start.1
  22.8 0.1 collective-permute-start.10
  22.9 0.6 %copy-done = s32[8]{0:T(128)S(1)} copy-done((s32[8]{0:T(128)S(1)}, s32[8]{0:T(128)}, u32[]{:S(2)}) %copy-start) | copy-done | bytes 56
  23.5 0.0 copy-done.1
  23.5 1.3 %shard_map.46 = (f32[512,256]{1,0:T(8,128)S(1)}, f32[512,256]{1,0:T(8,128)S(1)}) custom-call(s32[8]{0:T(128)S(1)} %copy-done, s32[8]{0:T(128)S(1)} %copy-done.1, f32[128,512]{1,0:T(8,128)S(1)} %pad_maximum_fusion.a_ref, f32[128,512]{1,0:T(8,128)S(1)} %collective-permute-done.3.ay_ref, f32[128,256]{1,0:T(8,128)S(1)} %get-tuple-element.33.refs_0_, ...), custom_call_target="tpu_custom_call" | custom-call | tf_op jit(solution)/shard_map/pallas_call | solution.py:148
  24.8 0.6 %collective-permute-done.8.my_ref = f32[256,256]{1,0:T(8,128)S(1)} collective-permute-done((f32[256,256]{1,0:T(8,128)S(1)}, f32[256,256]{1,0:T(8,128)S(1)}, u32[]{:S(2)}, u32[]{:S(2)}) %collective-permute-start.8) | collective-permute-done | bytes 262176 | tf_op jit(solution)/shard_map/ppermute | solution.py:106
  25.4 0.0 collective-permute-done.10.ack_ref
  25.4 1.2 %shard_map.47 = f32[512,256]{1,0:T(8,128)} custom-call(f32[512,256]{1,0:T(8,128)S(1)} %get-tuple-element.10.part_ref, f32[512,256]{1,0:T(8,128)S(1)} %get-tuple-element.11.mask_ref, f32[256,256]{1,0:T(8,128)S(1)} %collective-permute-done.8.my_ref, f32[256,256]{1,0:T(8,128)S(1)} %maximum_select_fusion.acx_ref, ...), custom_call_target="tpu_custom_call" | custom-call | tf_op jit(solution)/shard_map/pallas_call | solution.py:162
  (16 shorter events, 0.2 us)
Async XLA Ops:
  0.0 9.8 %collective-permute-start.2 = (f32[32,512]{1,0:T(8,128)}, f32[32,512]{1,0:T(8,128)S(1)}, u32[]{:S(2)}, u32[]{:S(2)}) collective-permute-start(f32[32,512]{1,0:T(8,128)} %bitcast.6), channel_id=1, source_target_pairs={{0,6},{1,7},{2,4},{3,5},{4,2},{5,3},{6,0},{7,1},{8,14},{9,15},{10,... | collective-permute-start | bytes 196616 | tf_op jit(solution)/shard_map/ppermute | solution.py:106
  5.0 5.8 %collective-permute-start.1 = (f32[32,512]{1,0:T(8,128)}, f32[32,512]{1,0:T(8,128)S(1)}, u32[]{:S(2)}, u32[]{:S(2)}) collective-permute-start(f32[32,512]{1,0:T(8,128)} %bitcast.7), channel_id=1, source_target_pairs={{0,4},{1,5},{2,6},{3,7},{4,0},{5,1},{6,2},{7,3},{8,12},{9,13},{10,... | collective-permute-start | bytes 196616 | tf_op jit(solution)/shard_map/ppermute | solution.py:106
  5.1 5.8 %collective-permute-start = (f32[32,512]{1,0:T(8,128)}, f32[32,512]{1,0:T(8,128)S(1)}, u32[]{:S(2)}, u32[]{:S(2)}) collective-permute-start(f32[32,512]{1,0:T(8,128)} %bitcast.8), channel_id=1, source_target_pairs={{0,2},{1,3},{2,0},{3,1},{4,6},{5,7},{6,4},{7,5},{8,10},{9,11},{10,... | collective-permute-start | bytes 196616 | tf_op jit(solution)/shard_map/ppermute | solution.py:106
  5.6 1.5 %collective-permute-start.4 = (f32[64,256]{1,0:T(8,128)}, f32[64,256]{1,0:T(8,128)S(1)}, u32[]{:S(2)}, u32[]{:S(2)}) collective-permute-start(f32[64,256]{1,0:T(8,128)} %param.5), channel_id=1, source_target_pairs={{0,8},{1,9},{2,10},{3,11},{4,12},{5,13},{6,14},{7,15},{8,0},{9,1},... | collective-permute-start | bytes 196616 | tf_op jit(solution)/shard_map/ppermute | solution.py:106
  5.6 0.9 %copy-start.2 = (f32[512,32]{0,1:T(8,128)S(1)}, f32[512,32]{0,1:T(8,128)}, u32[]{:S(2)}) copy-start(f32[512,32]{0,1:T(8,128)} %param.4) | copy-start | bytes 196612
  7.1 9.7 %collective-permute-start.7 = (f32[128,256]{1,0:T(8,128)S(1)}, f32[128,256]{1,0:T(8,128)S(1)}, u32[]{:S(2)}, u32[]{:S(2)}) collective-permute-start(f32[128,256]{1,0:T(8,128)S(1)} %get-tuple-element.33.refs_0_), channel_id=1, source_target_pairs={{0,4},{1,5},{2,12},{3,13},{4,20},{5,21},{6,28},{7,29},{8,6},{9,7},... | collective-permute-start | bytes 393224 | tf_op jit(solution)/shard_map/ppermute | solution.py:106
  9.5 7.3 %collective-permute-start.6 = (f32[128,256]{1,0:T(8,128)S(1)}, f32[128,256]{1,0:T(8,128)S(1)}, u32[]{:S(2)}, u32[]{:S(2)}) collective-permute-start(f32[128,256]{1,0:T(8,128)S(1)} %get-tuple-element.33.refs_0_), channel_id=1, source_target_pairs={{0,2},{1,3},{2,10},{3,11},{4,18},{5,19},{6,26},{7,27},{8,0},{9,1},... | collective-permute-start | bytes 393224 | tf_op jit(solution)/shard_map/ppermute | solution.py:106
  10.9 8.5 %collective-permute-start.3 = (f32[128,512]{1,0:T(8,128)S(1)}, f32[128,512]{1,0:T(8,128)S(1)}, u32[]{:S(2)}, u32[]{:S(2)}) collective-permute-start(f32[128,512]{1,0:T(8,128)S(1)} %pad_maximum_fusion.a_ref), channel_id=1, source_target_pairs={{0,1},{1,0},{2,3},{3,2},{4,5},{5,4},{6,7},{7,6},{8,9},{9,8},{10,11... | collective-permute-start | bytes 786440 | tf_op jit(solution)/shard_map/ppermute | solution.py:106
  12.5 8.8 %collective-permute-start.5 = (f32[256,256]{1,0:T(8,128)S(1)}, f32[256,256]{1,0:T(8,128)S(1)}, u32[]{:S(2)}, u32[]{:S(2)}) collective-permute-start(f32[256,256]{1,0:T(8,128)S(1)} %get-tuple-element.29), channel_id=1, source_target_pairs={{0,16},{1,17},{2,18},{3,19},{4,20},{5,21},{6,22},{7,23},{8,24},{9,... | collective-permute-start | bytes 786440 | tf_op jit(solution)/shard_map/ppermute | solution.py:106
  14.9 7.9 %collective-permute-start.9 = (f32[128,256]{1,0:T(8,128)S(1)}, f32[128,256]{1,0:T(8,128)S(1)}, u32[]{:S(2)}, u32[]{:S(2)}) collective-permute-start(f32[128,256]{1,0:T(8,128)S(1)} %pad_maximum_fusion.2), channel_id=1, source_target_pairs={{0,17},{1,16},{10,27},{11,26},{20,5},{21,4},{30,15},{31,14}} | collective-permute-start | bytes 393224 | tf_op jit(solution)/shard_map/ppermute | solution.py:106
  16.8 8.5 %collective-permute-start.8 = (f32[256,256]{1,0:T(8,128)S(1)}, f32[256,256]{1,0:T(8,128)S(1)}, u32[]{:S(2)}, u32[]{:S(2)}) collective-permute-start(f32[256,256]{1,0:T(8,128)S(1)} %pad_maximum_fusion.1), channel_id=1, source_target_pairs={{0,1},{1,0},{2,3},{3,2},{4,5},{5,4},{6,7},{7,6},{8,9},{9,8},{10,11... | collective-permute-start | bytes 786440 | tf_op jit(solution)/shard_map/ppermute | solution.py:106
  22.8 0.7 %copy-start = (s32[8]{0:T(128)S(1)}, s32[8]{0:T(128)}, u32[]{:S(2)}) copy-start(s32[8]{0:T(128)} %occ_hbm.1) | copy-start | bytes 100
  22.8 0.7 %copy-start.1 = (s32[8]{0:T(128)S(1)}, s32[8]{0:T(128)}, u32[]{:S(2)}) copy-start(s32[8]{0:T(128)} %vir_hbm.1) | copy-start | bytes 100
  22.8 2.5 %collective-permute-start.10 = (f32[256,256]{1,0:T(8,128)S(1)}, f32[256,256]{1,0:T(8,128)S(1)}, u32[]{:S(2)}, u32[]{:S(2)}) collective-permute-start(f32[256,256]{1,0:T(8,128)S(1)} %maximum_select_fusion.acx_ref), channel_id=1, source_target_pairs={{0,8},{1,9},{2,10},{3,11},{4,12},{5,13},{6,14},{7,15},{8,0},{9,1},... | collective-permute-start | bytes 786440 | tf_op jit(solution)/shard_map/ppermute | solution.py:106

commit v7 on v6

--- a/solution.py
+++ b/solution.py
@@ -68,7 +68,7 @@
         vir.append(two)
     rows = labels_of(row * tall + lax.broadcasted_iota(jnp.int32, (tall, 1), 0), occ, vir)
     cols = labels_of(col * narrow + lax.broadcasted_iota(jnp.int32, (1, narrow), 1), occ, vir)
-    mask_ref[...] = jnp.where(rows == cols, 1.0, 0.0)
+    mask_ref[...] = jnp.where(rows == cols, 1.0, 0.0).astype(jnp.bfloat16)
 
 
 def mirrored(sizes, part_ref, mask_ref, my_ref, acx_ref, ack_ref, *refs):
@@ -89,7 +89,7 @@
     for half, left in enumerate((jnp.concatenate([m_ref[...] for m_ref in m_refs], axis=0), my_ref[...])):
         rows = pl.ds(pl.multiple_of((y ^ half) * narrow, narrow), narrow)
         total = part_ref[rows, :] + product(halves(left), right_halves)
-        done[half] = jnp.where(mask_ref[rows, :] > 0.0, total, 0.0)
+        done[half] = jnp.where(mask_ref[rows, :].astype(jnp.float32) > 0.0, total, 0.0)
         stores.append(pltpu.make_async_copy(done.at[half], out_hbm.at[rows, :], sems.at[half]))
         stores[half].start()
     for store in stores:
@@ -147,7 +147,7 @@
     tile = jax.ShapeDtypeStruct((tall, narrow), jnp.float32)
     part, mask = pl.pallas_call(
         functools.partial(direct, sizes),
-        out_shape=(tile, tile),
+        out_shape=(tile, jax.ShapeDtypeStruct((tall, narrow), jnp.bfloat16)),
         in_specs=[hbm, hbm] + [vmem] * (2 + nr // 2),
         out_specs=(vmem, vmem),
         scratch_shapes=[

time: 26.8 us -> 26.8 us (level)
  no operation moved by 1% of the time
where the time goes in v7:
time: 26.8 us; the launch traced here: 26.6 us
  starting transfers between devices  15.8 us (59%)
  waiting for transfers between devices  6.4 us (24%)
  Pallas kernels  2.5 us (9%)
  local copies, waits for them, and re-layouts  1.6 us (6%)
    ppermute x11, starting transfers between devices, send(): return lax.ppermute(value, ('row', 'col'), pairs)  15.8 us
    ppermute x11, waiting for transfers between devices, send(): return lax.ppermute(value, ('row', 'col'), pairs)  6.4 us
    unnamed x12, local copies, waits for them, and re-layouts  1.51 us
    pallas_call x1, Pallas kernels, per_device(): pl.pallas_call(functools.partial(direct, sizes), out_shape=(tile, jax.Sha...  1.27 us
    pallas_call x1, Pallas kernels, per_device(): pl.pallas_call(functools.partial(mirrored, sizes), out_shape=tile, in_spe...  1.23 us
  transfers between devices with their start and end apart: 11, of which 6 were waited for; matrix products, arithmetic and copies ran while one was open for 4% of the time, Pallas kernels for 5%

profile of v7, /device:TPU:0, one launch (start us, length us, event | category | flops | bytes accessed | tf_op | source)
XLA Modules:
  0.0 26.6 jit_solution(9016452367558040341)
XLA Ops:
  0.0 5.0 %collective-permute-start.2 = (f32[32,512]{1,0:T(8,128)}, f32[32,512]{1,0:T(8,128)S(1)}, u32[]{:S(2)}, u32[]{:S(2)}) collective-permute-start(f32[32,512]{1,0:T(8,128)} %bitcast.6), channel_id=1, source_target_pairs={{0,6},{1,7},{2,4},{3,5},{4,2},{5,3},{6,0},{7,1},{8,14},{9,15},{10,... | collective-permute-start | bytes 196616 | tf_op jit(solution)/shard_map/ppermute | solution.py:106
  5.0 0.0 collective-permute-start.1
  5.1 0.6 %collective-permute-start = (f32[32,512]{1,0:T(8,128)}, f32[32,512]{1,0:T(8,128)S(1)}, u32[]{:S(2)}, u32[]{:S(2)}) collective-permute-start(f32[32,512]{1,0:T(8,128)} %bitcast.8), channel_id=1, source_target_pairs={{0,2},{1,3},{2,0},{3,1},{4,6},{5,7},{6,4},{7,5},{8,10},{9,11},{10,... | collective-permute-start | bytes 196616 | tf_op jit(solution)/shard_map/ppermute | solution.py:106
  5.6 0.0 collective-permute-start.4
  5.6 0.0 copy-start.2
  5.6 0.9 %constant_dynamic-update-slice_fusion.7 = (f32[256,256]{1,0:T(8,128)S(1)}, f32[128,256]{1,0:T(8,128)S(1)}) fusion(f32[64,256]{1,0:T(8,128)} %param.5), kind=kLoop, calls=%fused_computation.12 | loop fusion | bytes 196608
  6.5 0.0 copy-done.2
  6.6 0.5 %collective-permute-done.4 = f32[64,256]{1,0:T(8,128)S(1)} collective-permute-done((f32[64,256]{1,0:T(8,128)}, f32[64,256]{1,0:T(8,128)S(1)}, u32[]{:S(2)}, u32[]{:S(2)}) %collective-permute-start.4) | collective-permute-done | bytes 65568 | tf_op jit(solution)/shard_map/ppermute | solution.py:106
  7.1 2.4 %collective-permute-start.7 = (f32[128,256]{1,0:T(8,128)S(1)}, f32[128,256]{1,0:T(8,128)S(1)}, u32[]{:S(2)}, u32[]{:S(2)}) collective-permute-start(f32[128,256]{1,0:T(8,128)S(1)} %get-tuple-element.33.refs_0_), channel_id=1, source_target_pairs={{0,4},{1,5},{2,12},{3,13},{4,20},{5,21},{6,28},{7,29},{8,6},{9,7},... | collective-permute-start | bytes 393224 | tf_op jit(solution)/shard_map/ppermute | solution.py:106
  9.5 0.3 %collective-permute-start.6 = (f32[128,256]{1,0:T(8,128)S(1)}, f32[128,256]{1,0:T(8,128)S(1)}, u32[]{:S(2)}, u32[]{:S(2)}) collective-permute-start(f32[128,256]{1,0:T(8,128)S(1)} %get-tuple-element.33.refs_0_), channel_id=1, source_target_pairs={{0,2},{1,3},{2,10},{3,11},{4,18},{5,19},{6,26},{7,27},{8,0},{9,1},... | collective-permute-start | bytes 393224 | tf_op jit(solution)/shard_map/ppermute | solution.py:106
  9.8 0.0 collective-permute-done.2
  9.8 1.0 %collective-permute-done.1 = f32[32,512]{1,0:T(8,128)S(1)} collective-permute-done((f32[32,512]{1,0:T(8,128)}, f32[32,512]{1,0:T(8,128)S(1)}, u32[]{:S(2)}, u32[]{:S(2)}) %collective-permute-start.1) | collective-permute-done | bytes 65568 | tf_op jit(solution)/shard_map/ppermute | solution.py:106
  10.9 0.0 collective-permute-done
  10.9 1.6 %collective-permute-start.3 = (f32[128,512]{1,0:T(8,128)S(1)}, f32[128,512]{1,0:T(8,128)S(1)}, u32[]{:S(2)}, u32[]{:S(2)}) collective-permute-start(f32[128,512]{1,0:T(8,128)S(1)} %pad_maximum_fusion.a_ref), channel_id=1, source_target_pairs={{0,1},{1,0},{2,3},{3,2},{4,5},{5,4},{6,7},{7,6},{8,9},{9,8},{10,11... | collective-permute-start | bytes 786440 | tf_op jit(solution)/shard_map/ppermute | solution.py:106
  12.5 2.3 %collective-permute-start.5 = (f32[256,256]{1,0:T(8,128)S(1)}, f32[256,256]{1,0:T(8,128)S(1)}, u32[]{:S(2)}, u32[]{:S(2)}) collective-permute-start(f32[256,256]{1,0:T(8,128)S(1)} %get-tuple-element.29), channel_id=1, source_target_pairs={{0,16},{1,17},{2,18},{3,19},{4,20},{5,21},{6,22},{7,23},{8,24},{9,... | collective-permute-start | bytes 786440 | tf_op jit(solution)/shard_map/ppermute | solution.py:106
  14.9 1.9 %collective-permute-start.9 = (f32[128,256]{1,0:T(8,128)S(1)}, f32[128,256]{1,0:T(8,128)S(1)}, u32[]{:S(2)}, u32[]{:S(2)}) collective-permute-start(f32[128,256]{1,0:T(8,128)S(1)} %pad_maximum_fusion.2), channel_id=1, source_target_pairs={{0,17},{1,16},{10,27},{11,26},{20,5},{21,4},{30,15},{31,14}} | collective-permute-start | bytes 393224 | tf_op jit(solution)/shard_map/ppermute | solution.py:106
  16.8 0.0 collective-permute-done.7.refs_1_
  16.8 0.0 collective-permute-done.6.refs_0_
  16.8 1.6 %collective-permute-start.8 = (f32[256,256]{1,0:T(8,128)S(1)}, f32[256,256]{1,0:T(8,128)S(1)}, u32[]{:S(2)}, u32[]{:S(2)}) collective-permute-start(f32[256,256]{1,0:T(8,128)S(1)} %pad_maximum_fusion.1), channel_id=1, source_target_pairs={{0,1},{1,0},{2,3},{3,2},{4,5},{5,4},{6,7},{7,6},{8,9},{9,8},{10,11... | collective-permute-start | bytes 786440 | tf_op jit(solution)/shard_map/ppermute | solution.py:106
  18.4 1.0 %collective-permute-done.3.ay_ref = f32[128,512]{1,0:T(8,128)S(1)} collective-permute-done((f32[128,512]{1,0:T(8,128)S(1)}, f32[128,512]{1,0:T(8,128)S(1)}, u32[]{:S(2)}, u32[]{:S(2)}) %collective-permute-start.3) | collective-permute-done | bytes 262176 | tf_op jit(solution)/shard_map/ppermute | solution.py:106
  19.5 1.9 %collective-permute-done.5 = f32[256,256]{1,0:T(8,128)S(1)} collective-permute-done((f32[256,256]{1,0:T(8,128)S(1)}, f32[256,256]{1,0:T(8,128)S(1)}, u32[]{:S(2)}, u32[]{:S(2)}) %collective-permute-start.5) | collective-permute-done | bytes 262176 | tf_op jit(solution)/shard_map/ppermute | solution.py:106
  21.4 1.3 %collective-permute-done.9 = f32[128,256]{1,0:T(8,128)S(1)} collective-permute-done((f32[128,256]{1,0:T(8,128)S(1)}, f32[128,256]{1,0:T(8,128)S(1)}, u32[]{:S(2)}, u32[]{:S(2)}) %collective-permute-start.9) | collective-permute-done | bytes 131104 | tf_op jit(solution)/shard_map/ppermute | solution.py:106
  22.8 0.0 copy-start
  22.8 0.0 copy-start.1
  22.8 0.1 collective-permute-start.10
  22.9 0.6 %copy-done = s32[8]{0:T(128)S(1)} copy-done((s32[8]{0:T(128)S(1)}, s32[8]{0:T(128)}, u32[]{:S(2)}) %copy-start) | copy-done | bytes 56
  23.5 0.0 copy-done.1
  23.5 1.3 %shard_map.46 = (f32[512,256]{1,0:T(8,128)S(1)}, bf16[512,256]{1,0:T(8,128)(2,1)S(1)}) custom-call(s32[8]{0:T(128)S(1)} %copy-done, s32[8]{0:T(128)S(1)} %copy-done.1, f32[128,512]{1,0:T(8,128)S(1)} %pad_maximum_fusion.a_ref, f32[128,512]{1,0:T(8,128)S(1)} %collective-permute-done.3.ay_ref, f32[128,256]{1,0:T(8,128)S(1)} %get-tuple-element.33.refs_0_, ...), custom_call_target="tpu_custom_call" | custom-call | tf_op jit(solution)/shard_map/pallas_call | solution.py:148
  24.8 0.6 %collective-permute-done.8.my_ref = f32[256,256]{1,0:T(8,128)S(1)} collective-permute-done((f32[256,256]{1,0:T(8,128)S(1)}, f32[256,256]{1,0:T(8,128)S(1)}, u32[]{:S(2)}, u32[]{:S(2)}) %collective-permute-start.8) | collective-permute-done | bytes 262176 | tf_op jit(solution)/shard_map/ppermute | solution.py:106
  25.4 0.0 collective-permute-done.10.ack_ref
  25.4 1.2 %shard_map.47 = f32[512,256]{1,0:T(8,128)} custom-call(f32[512,256]{1,0:T(8,128)S(1)} %get-tuple-element.10.part_ref, bf16[512,256]{1,0:T(8,128)(2,1)S(1)} %get-tuple-element.11.mask_ref, f32[256,256]{1,0:T(8,128)S(1)} %collective-permute-done.8.my_ref, f32[256,256]{1,0:T(8,128)S(1)} %maximum_select_fusion.acx_ref, ...), custom_call_target="tpu_custom_call" | custom-call | tf_op jit(solution)/shard_map/pallas_call | solution.py:162
  (16 shorter events, 0.2 us)
Async XLA Ops:
  0.0 9.8 %collective-permute-start.2 = (f32[32,512]{1,0:T(8,128)}, f32[32,512]{1,0:T(8,128)S(1)}, u32[]{:S(2)}, u32[]{:S(2)}) collective-permute-start(f32[32,512]{1,0:T(8,128)} %bitcast.6), channel_id=1, source_target_pairs={{0,6},{1,7},{2,4},{3,5},{4,2},{5,3},{6,0},{7,1},{8,14},{9,15},{10,... | collective-permute-start | bytes 196616 | tf_op jit(solution)/shard_map/ppermute | solution.py:106
  5.0 5.8 %collective-permute-start.1 = (f32[32,512]{1,0:T(8,128)}, f32[32,512]{1,0:T(8,128)S(1)}, u32[]{:S(2)}, u32[]{:S(2)}) collective-permute-start(f32[32,512]{1,0:T(8,128)} %bitcast.7), channel_id=1, source_target_pairs={{0,4},{1,5},{2,6},{3,7},{4,0},{5,1},{6,2},{7,3},{8,12},{9,13},{10,... | collective-permute-start | bytes 196616 | tf_op jit(solution)/shard_map/ppermute | solution.py:106
  5.1 5.8 %collective-permute-start = (f32[32,512]{1,0:T(8,128)}, f32[32,512]{1,0:T(8,128)S(1)}, u32[]{:S(2)}, u32[]{:S(2)}) collective-permute-start(f32[32,512]{1,0:T(8,128)} %bitcast.8), channel_id=1, source_target_pairs={{0,2},{1,3},{2,0},{3,1},{4,6},{5,7},{6,4},{7,5},{8,10},{9,11},{10,... | collective-permute-start | bytes 196616 | tf_op jit(solution)/shard_map/ppermute | solution.py:106
  5.6 1.5 %collective-permute-start.4 = (f32[64,256]{1,0:T(8,128)}, f32[64,256]{1,0:T(8,128)S(1)}, u32[]{:S(2)}, u32[]{:S(2)}) collective-permute-start(f32[64,256]{1,0:T(8,128)} %param.5), channel_id=1, source_target_pairs={{0,8},{1,9},{2,10},{3,11},{4,12},{5,13},{6,14},{7,15},{8,0},{9,1},... | collective-permute-start | bytes 196616 | tf_op jit(solution)/shard_map/ppermute | solution.py:106
  5.6 0.9 %copy-start.2 = (f32[512,32]{0,1:T(8,128)S(1)}, f32[512,32]{0,1:T(8,128)}, u32[]{:S(2)}) copy-start(f32[512,32]{0,1:T(8,128)} %param.4) | copy-start | bytes 196612
  7.1 9.7 %collective-permute-start.7 = (f32[128,256]{1,0:T(8,128)S(1)}, f32[128,256]{1,0:T(8,128)S(1)}, u32[]{:S(2)}, u32[]{:S(2)}) collective-permute-start(f32[128,256]{1,0:T(8,128)S(1)} %get-tuple-element.33.refs_0_), channel_id=1, source_target_pairs={{0,4},{1,5},{2,12},{3,13},{4,20},{5,21},{6,28},{7,29},{8,6},{9,7},... | collective-permute-start | bytes 393224 | tf_op jit(solution)/shard_map/ppermute | solution.py:106
  9.5 7.3 %collective-permute-start.6 = (f32[128,256]{1,0:T(8,128)S(1)}, f32[128,256]{1,0:T(8,128)S(1)}, u32[]{:S(2)}, u32[]{:S(2)}) collective-permute-start(f32[128,256]{1,0:T(8,128)S(1)} %get-tuple-element.33.refs_0_), channel_id=1, source_target_pairs={{0,2},{1,3},{2,10},{3,11},{4,18},{5,19},{6,26},{7,27},{8,0},{9,1},... | collective-permute-start | bytes 393224 | tf_op jit(solution)/shard_map/ppermute | solution.py:106
  10.9 8.5 %collective-permute-start.3 = (f32[128,512]{1,0:T(8,128)S(1)}, f32[128,512]{1,0:T(8,128)S(1)}, u32[]{:S(2)}, u32[]{:S(2)}) collective-permute-start(f32[128,512]{1,0:T(8,128)S(1)} %pad_maximum_fusion.a_ref), channel_id=1, source_target_pairs={{0,1},{1,0},{2,3},{3,2},{4,5},{5,4},{6,7},{7,6},{8,9},{9,8},{10,11... | collective-permute-start | bytes 786440 | tf_op jit(solution)/shard_map/ppermute | solution.py:106
  12.5 8.8 %collective-permute-start.5 = (f32[256,256]{1,0:T(8,128)S(1)}, f32[256,256]{1,0:T(8,128)S(1)}, u32[]{:S(2)}, u32[]{:S(2)}) collective-permute-start(f32[256,256]{1,0:T(8,128)S(1)} %get-tuple-element.29), channel_id=1, source_target_pairs={{0,16},{1,17},{2,18},{3,19},{4,20},{5,21},{6,22},{7,23},{8,24},{9,... | collective-permute-start | bytes 786440 | tf_op jit(solution)/shard_map/ppermute | solution.py:106
  14.9 7.9 %collective-permute-start.9 = (f32[128,256]{1,0:T(8,128)S(1)}, f32[128,256]{1,0:T(8,128)S(1)}, u32[]{:S(2)}, u32[]{:S(2)}) collective-permute-start(f32[128,256]{1,0:T(8,128)S(1)} %pad_maximum_fusion.2), channel_id=1, source_target_pairs={{0,17},{1,16},{10,27},{11,26},{20,5},{21,4},{30,15},{31,14}} | collective-permute-start | bytes 393224 | tf_op jit(solution)/shard_map/ppermute | solution.py:106
  16.8 8.5 %collective-permute-start.8 = (f32[256,256]{1,0:T(8,128)S(1)}, f32[256,256]{1,0:T(8,128)S(1)}, u32[]{:S(2)}, u32[]{:S(2)}) collective-permute-start(f32[256,256]{1,0:T(8,128)S(1)} %pad_maximum_fusion.1), channel_id=1, source_target_pairs={{0,1},{1,0},{2,3},{3,2},{4,5},{5,4},{6,7},{7,6},{8,9},{9,8},{10,11... | collective-permute-start | bytes 786440 | tf_op jit(solution)/shard_map/ppermute | solution.py:106
  22.8 0.7 %copy-start = (s32[8]{0:T(128)S(1)}, s32[8]{0:T(128)}, u32[]{:S(2)}) copy-start(s32[8]{0:T(128)} %occ_hbm.1) | copy-start | bytes 100
  22.8 0.7 %copy-start.1 = (s32[8]{0:T(128)S(1)}, s32[8]{0:T(128)}, u32[]{:S(2)}) copy-start(s32[8]{0:T(128)} %vir_hbm.1) | copy-start | bytes 100
  22.8 2.5 %collective-permute-start.10 = (f32[256,256]{1,0:T(8,128)S(1)}, f32[256,256]{1,0:T(8,128)S(1)}, u32[]{:S(2)}, u32[]{:S(2)}) collective-permute-start(f32[256,256]{1,0:T(8,128)S(1)} %maximum_select_fusion.acx_ref), channel_id=1, source_target_pairs={{0,8},{1,9},{2,10},{3,11},{4,12},{5,13},{6,14},{7,15},{8,0},{9,1},... | collective-permute-start | bytes 786440 | tf_op jit(solution)/shard_map/ppermute | solution.py:106
